TPU v7x, 256 devices: a whole 4x4x8 slice. The times are simulated.
256 devices in a mesh: dp: 4 (over x_lo, core), expert: 64 (over z, y, x_hi).
Axes of the slice: x: 4 (x_hi: 2, x_lo: 2; x = x_hi * 2 + x_lo), y: 4, z: 8, core: 2. Of those that a mesh axis runs over, the one named last changes fastest.
Arguments:
- tokens: bfloat16 [40960, 2048], P(('dp', 'expert')), may hold values from -6 to 6
- routes: int32 [40960, 2], P(('dp', 'expert')), may hold values from 0 to 63, all different within a row
- gate_probs: float32 [40960, 2], P(('dp', 'expert')), may hold values from 0.1 to 1
- cotangent: bfloat16 [40960, 2048], P(('dp', 'expert')), may hold values from -6 to 6
- w_gate: bfloat16 [64, 2048, 768], P('expert', 'dp'), may hold values from -0.125 to 0.125
- w_up: bfloat16 [64, 2048, 768], P('expert', 'dp'), may hold values from -0.125 to 0.125
- w_down: bfloat16 [64, 768, 2048], P('expert', None, 'dp'), may hold values from -0.21875 to 0.21875
Outputs:
- layer_out: bfloat16 [40960, 2048], P(('dp', 'expert'))
- d_tokens: bfloat16 [40960, 2048], P(('dp', 'expert'))
- d_gates: float32 [40960, 2], P(('dp', 'expert'))
- grad_gate: float32 [64, 2048, 768], P('expert', 'dp')
- grad_up: float32 [64, 2048, 768], P('expert', 'dp')
- grad_down: float32 [64, 768, 2048], P('expert', None, 'dp')
Inputs may be any that keep to these rules, and one draw needn't show every extreme that they name: `routes`: each row names 2 different experts; every expert is named by some row.
All inputs are finite; a program needn't handle non-finite values.
Results may differ from a plain program's by a relative error of at most 0.0065.
Values may be sent and summed in bfloat16 or wider, within the bound.
A program may use at most 128 MiB of HBM per device.

v0:
```python
from functools import reduce

import jax
import jax.numpy as jnp
from jax import lax
from jax.sharding import PartitionSpec as P


def silu_parts(pre_act):
    sig_value = jax.nn.sigmoid(pre_act)
    return (pre_act * sig_value, sig_value * (1.0 + pre_act * (1.0 - sig_value)))


def contract_rows(first_op, second_op):
    return lax.dot_general(
        first_op, second_op, (((0,), (0,)), ((), ())), preferred_element_type=jnp.float32
    )


def contract_last(first_op, second_op):
    return lax.dot_general(
        first_op, second_op, (((1,), (1,)), ((), ())), preferred_element_type=jnp.float32
    )


def expert_forward(flat_rows, weights):
    gate_mat, up_mat, down_mat = weights
    gate_pre = jnp.dot(flat_rows, gate_mat, preferred_element_type=jnp.float32)
    up_pre = jnp.dot(flat_rows, up_mat, preferred_element_type=jnp.float32)
    active, unused_slope = silu_parts(gate_pre)
    hidden = (active * up_pre).astype(jnp.bfloat16)
    result = jnp.dot(hidden, down_mat, preferred_element_type=jnp.float32).astype(jnp.bfloat16)
    return (gate_pre, up_pre, hidden, result)


def expert_backward(route_grad, gate_pre, up_pre, weights):
    gate_mat, up_mat, down_mat = weights
    d_hidden = contract_last(route_grad, down_mat)
    active, silu_slope = silu_parts(gate_pre)
    d_gate = (d_hidden * up_pre * silu_slope).astype(jnp.bfloat16)
    d_up = (d_hidden * active).astype(jnp.bfloat16)
    d_rows = (contract_last(d_gate, gate_mat) + contract_last(d_up, up_mat)).astype(jnp.bfloat16)
    return (d_gate, d_up, d_rows)


def on_device(tokens, routes, gate_probs, cotangent, w_gate, w_up, w_down):
    tok_count, model_width = tokens.shape
    fanout = routes.shape[1]
    experts = lax.axis_size("expert") * w_gate.shape[0]
    capacity = max(2, 3 * tok_count * fanout // (2 * experts))
    slots_all = experts * capacity
    full_gate, full_up, full_down = (
        lax.all_gather(w_gate, "dp", axis=1, tiled=True),
        lax.all_gather(w_up, "dp", axis=1, tiled=True),
        lax.all_gather(w_down, "dp", axis=2, tiled=True),
    )
    weights = (full_gate[0], full_up[0], full_down[0])
    hidden_width = weights[0].shape[1]
    expert_hits = (
        (routes[:, :, None] == jnp.arange(experts, dtype=jnp.int32)[None, None, :])
        .astype(jnp.int32)
        .sum(1)
    )
    before = jnp.cumsum(expert_hits, axis=0) - expert_hits
    slot_rank = jnp.take_along_axis(before, routes, axis=1)
    is_kept = slot_rank < capacity
    slot_index = jnp.where(is_kept, routes * capacity + slot_rank, slots_all)
    slot_ids = jnp.arange(slots_all, dtype=jnp.int32)[:, None]
    pickers = [
        (slot_index[:, route][None, :] == slot_ids).astype(jnp.bfloat16) for route in range(fanout)
    ]
    picker = reduce(jnp.add, pickers)
    x_slots = jnp.dot(picker, tokens, preferred_element_type=jnp.float32).astype(jnp.bfloat16)
    x_slots = x_slots.reshape(experts, capacity, model_width)
    grad_wide = cotangent.astype(jnp.float32)
    route_grads = [
        (gate_probs[:, route : route + 1] * grad_wide).astype(jnp.bfloat16)
        for route in range(fanout)
    ]
    grad_terms = [
        jnp.dot(pickers[route], route_grads[route], preferred_element_type=jnp.float32)
        for route in range(fanout)
    ]
    g_slots = (
        reduce(jnp.add, grad_terms).astype(jnp.bfloat16).reshape(experts, capacity, model_width)
    )
    received = lax.all_to_all(x_slots, "expert", split_axis=0, concat_axis=0, tiled=True)
    item_shape = received.shape
    lead_dims = (item_shape[0], item_shape[1], -1)
    flat_rows = received.reshape(-1, model_width)
    gate_pre, up_pre, hidden, result = expert_forward(flat_rows, weights)
    out_back = lax.all_to_all(
        result.reshape(item_shape), "expert", split_axis=0, concat_axis=0, tiled=True
    )
    out_back, received, gate_pre, up_pre, hidden = (
        out_back,
        received,
        gate_pre.reshape(lead_dims),
        up_pre.reshape(lead_dims),
        hidden.reshape(lead_dims),
    )
    flat_x = received.reshape(-1, model_width)
    hidden = hidden.reshape(-1, hidden_width)
    incoming = lax.all_to_all(g_slots, "expert", split_axis=0, concat_axis=0, tiled=True).reshape(
        -1, model_width
    )
    d_gate, d_up, d_rows = expert_backward(
        incoming, gate_pre.reshape(-1, hidden_width), up_pre.reshape(-1, hidden_width), weights
    )
    dx_back = lax.all_to_all(
        d_rows.reshape(experts, capacity, model_width),
        "expert",
        split_axis=0,
        concat_axis=0,
        tiled=True,
    )
    part_gate = contract_rows(flat_x, d_gate)[None]
    part_up = contract_rows(flat_x, d_up)[None]
    part_down = contract_rows(hidden, incoming)[None]
    grad_gate, grad_up, grad_down = (
        lax.psum_scatter(part_gate, "dp", scatter_dimension=1, tiled=True),
        lax.psum_scatter(part_up, "dp", scatter_dimension=1, tiled=True),
        lax.psum_scatter(part_down, "dp", scatter_dimension=2, tiled=True),
    )
    zero_row = jnp.zeros((1, model_width), jnp.bfloat16)
    out_pad = jnp.concatenate([out_back.reshape(-1, model_width), zero_row], 0)
    dx_pad = jnp.concatenate([dx_back.reshape(-1, model_width), zero_row], 0)
    layer_sum = jnp.zeros((tok_count, model_width), jnp.float32)
    d_tok = jnp.zeros((tok_count, model_width), jnp.float32)
    columns = []
    for route in range(fanout):
        picked = jnp.take(out_pad, slot_index[:, route], axis=0).astype(jnp.float32)
        layer_sum = layer_sum + gate_probs[:, route : route + 1] * picked
        d_tok = d_tok + jnp.take(dx_pad, slot_index[:, route], axis=0).astype(jnp.float32)
        columns.append(jnp.sum(grad_wide * picked, axis=1))
    d_gates = jnp.stack(columns, 1)
    return (
        layer_sum.astype(jnp.bfloat16),
        d_tok.astype(jnp.bfloat16),
        d_gates,
        grad_gate,
        grad_up,
        grad_down,
    )


def solution(mesh):
    return jax.shard_map(
        on_device,
        mesh=mesh,
        in_specs=(
            P(("dp", "expert"), None),
            P(("dp", "expert"), None),
            P(("dp", "expert"), None),
            P(("dp", "expert"), None),
            P("expert", "dp", None),
            P("expert", "dp", None),
            P("expert", None, "dp"),
        ),
        out_specs=(
            P(("dp", "expert"), None),
            P(("dp", "expert"), None),
            P(("dp", "expert"), None),
            P("expert", "dp", None),
            P("expert", "dp", None),
            P("expert", None, "dp"),
        ),
        check_vma=False,
    )
```

profile of v0, /device:TPU:1, one launch (start us, length us, event | category | flops | bytes accessed | tf_op | source)
XLA Modules:
  0.0 441.8 jit_solution(4493106976694748711)
XLA Ops:
  7.2 0.0 copy-start
  7.2 0.0 all-gather.8.cloned.1.call-start
  7.2 0.7 all-gather.8.cloned.1.call-update
  7.9 0.0 all-gather.6.cloned.1.call-start
  8.0 0.7 all-gather.6.cloned.1.call-update
  8.7 0.7 convert_reduce_fusion
  9.4 0.1 copy.52
  9.5 0.6 reduce-window.6
  10.1 0.2 slice_reduce_fusion
  10.3 0.1 broadcast_add_fusion
  10.4 0.1 copy.55
  10.6 0.1 copy.53
  10.7 0.1 reshape.107
  10.9 2.5 gather_fusion
  13.4 0.1 reshape.110
  13.5 0.1 copy.54
  13.7 0.7 fusion.25
  14.4 0.8 add_convert_fusion.1
  15.2 1.6 reshape.71
  16.8 15.1 %all-to-all-start.2 = ((bf16[64,7,2048]{2,1,0:T(8,128)(2,1)}), bf16[64,7,2048]{2,1,0:T(8,128)(2,1)S(1)}, u32[]{:S(2)}, u32[]{:S(2)}) async-start(bf16[64,7,2048]{2,1,0:T(8,128)(2,1)} %reshape.71), calls=%async_computation.2 | async-start | bytes 4194304 | tf_op jit(solution)/shard_map/all_to_all | solution.py:104
  32.0 0.0 all-gather.4.cloned.1.call-start
  32.0 0.7 all-gather.4.cloned.1.call-update
  32.7 1.9 convolution_convert_fusion
  34.6 3.6 reshape.67
  38.2 42.5 %all-to-all-done.2 = bf16[64,7,2048]{2,1,0:T(8,128)(2,1)S(1)} async-done(((bf16[64,7,2048]{2,1,0:T(8,128)(2,1)}), bf16[64,7,2048]{2,1,0:T(8,128)(2,1)S(1)}, u32[]{:S(2)}, u32[]{:S(2)}) %all-to-all-start.2) | async-done | bytes 1835040 | tf_op jit(solution)/shard_map/all_to_all | solution.py:104
  80.7 9.2 %all-to-all-start = ((bf16[64,7,2048]{2,1,0:T(8,128)(2,1)}), bf16[64,7,2048]{2,1,0:T(8,128)(2,1)}, u32[]{:S(2)}, u32[]{:S(2)}) async-start(bf16[64,7,2048]{2,1,0:T(8,128)(2,1)} %reshape.67), calls=%async_computation | async-start | bytes 4194304 | tf_op jit(solution)/shard_map/all_to_all | solution.py:87
  89.9 0.2 reduce-scatter.4.cloned.1.call-start
  90.1 1.6 reshape.72
  91.8 46.6 %all-to-all-done = bf16[64,7,2048]{2,1,0:T(8,128)(2,1)} async-done(((bf16[64,7,2048]{2,1,0:T(8,128)(2,1)}), bf16[64,7,2048]{2,1,0:T(8,128)(2,1)}, u32[]{:S(2)}, u32[]{:S(2)}) %all-to-all-start) | async-done | bytes 1835040 | tf_op jit(solution)/shard_map/all_to_all | solution.py:87
  138.3 3.7 reshape.68
  142.1 4.6 %fusion = f32[448,768]{1,0:T(8,128)} fusion(bf16[448,2048]{1,0:T(8,128)(2,1)S(1)} %copy-done.3, bf16[1,768,2048]{2,1,0:T(8,128)(2,1)} %all-gather.8.cloned.1.call-done), kind=kOutput, calls=%fused_computation.10 | convolution fusion | flops 1409286144 | bytes 6356992 | tf_op jit(solution)/shard_map/dot_general | solution.py:21
  146.7 5.1 %fusion.6 = f32[448,768]{1,0:T(8,128)} fusion(bf16[448,2048]{1,0:T(8,128)(2,1)} %reshape.68, bf16[1,2048,768]{2,1,0:T(8,128)(2,1)} %all-gather.6.cloned.1.call-done), kind=kOutput, calls=%fused_computation.16 | convolution fusion | flops 1409286144 | bytes 6356992 | tf_op jit(solution)/shard_map/dot_general | solution.py:29
  151.8 31.0 %all-gather.4.cloned.1.call-done = bf16[1,2048,768]{2,1,0:T(8,128)(2,1)} async-done(((bf16[1,512,768]{2,1,0:T(8,128)(2,1)}), bf16[1,2048,768]{2,1,0:T(8,128)(2,1)}) %all-gather.4.cloned.1.call-update) | async-done | bytes 3145744 | tf_op jit(solution)/shard_map/all_gather | solution.py:53
  182.8 6.6 %multiply_convert_fusion.1 = (bf16[448,768]{1,0:T(8,128)(2,1)S(1)}, bf16[448,768]{1,0:T(8,128)(2,1)}, bf16[448,768]{1,0:T(8,128)(2,1)}) fusion(f32[448,768]{1,0:T(8,128)} %fusion, f32[448,768]{1,0:T(8,128)} %fusion.6, bf16[448,2048]{1,0:T(8,128)(2,1)} %reshape.68, bf16[1,2048,768]{2,1,0:T(8,128)(2,1)} %all-gather.4.cloned.1.call-done), kind=kOutput, calls=%fused_computation.31 | convolution fusion | flops 1414447104 | bytes 9797632 | tf_op jit(solution)/shard_map/dot_general | solution.py:28
  189.4 0.8 copy-done.8
  190.2 4.5 %convolution_bitcast_fusion.2 = f32[1,2048,768]{2,1,0:T(8,128)} fusion(bf16[448,2048]{1,0:T(8,128)(2,1)S(1)} %copy-done.4, bf16[448,768]{1,0:T(8,128)(2,1)S(1)} %get-tuple-element.9), kind=kOutput, calls=%fused_computation.7 | convolution fusion | flops 1409286144 | bytes 8814592 | tf_op jit(solution)/shard_map/dot_general | solution.py:15
  194.7 0.0 reduce-scatter.4.cloned.1.call-update
  194.8 0.0 reduce-scatter.6.cloned.1.call-start
  194.8 6.1 %convolution_bitcast_fusion.1 = f32[1,2048,768]{2,1,0:T(8,128)} fusion(bf16[448,2048]{1,0:T(8,128)(2,1)} %reshape.68, bf16[448,768]{1,0:T(8,128)(2,1)} %get-tuple-element.10), kind=kOutput, calls=%fused_computation.6 | convolution fusion | flops 1409286144 | bytes 8814592 | tf_op jit(solution)/shard_map/dot_general | solution.py:15
  200.9 0.0 reduce-scatter.6.cloned.1.call-update
  201.0 0.0 reduce-scatter.8.cloned.1.call-start
  201.0 5.5 %convolution_bitcast_fusion = f32[1,768,2048]{2,1,0:T(8,128)} fusion(bf16[448,768]{1,0:T(8,128)(2,1)} %get-tuple-element.11, bf16[448,2048]{1,0:T(8,128)(2,1)S(1)} %copy-done.3), kind=kOutput, calls=%fused_computation.5 | convolution fusion | flops 1409286144 | bytes 8814592 | tf_op jit(solution)/shard_map/dot_general | solution.py:15
  206.5 0.0 reduce-scatter.8.cloned.1.call-update
  206.5 4.3 fusion.12
  210.9 1.7 reshape.69
  212.6 13.0 %all-to-all-start.1 = ((bf16[64,7,2048]{2,1,0:T(8,128)(2,1)}), bf16[64,7,2048]{2,1,0:T(8,128)(2,1)S(1)}, u32[]{:S(2)}, u32[]{:S(2)}) async-start(bf16[64,7,2048]{2,1,0:T(8,128)(2,1)} %reshape.69), calls=%async_computation.1 | async-start | bytes 4194304 | tf_op jit(solution)/shard_map/all_to_all | solution.py:92
  225.5 3.9 fusion.4
  229.4 2.9 add_convert_fusion
  232.3 3.6 reshape.73
  235.9 40.8 %all-to-all-done.1 = bf16[64,7,2048]{2,1,0:T(8,128)(2,1)S(1)} async-done(((bf16[64,7,2048]{2,1,0:T(8,128)(2,1)}), bf16[64,7,2048]{2,1,0:T(8,128)(2,1)S(1)}, u32[]{:S(2)}, u32[]{:S(2)}) %all-to-all-start.1) | async-done | bytes 1835040 | tf_op jit(solution)/shard_map/all_to_all | solution.py:92
  276.7 7.4 %all-to-all-start.3 = ((bf16[64,7,2048]{2,1,0:T(8,128)(2,1)}), bf16[64,7,2048]{2,1,0:T(8,128)(2,1)}, u32[]{:S(2)}, u32[]{:S(2)}) async-start(bf16[64,7,2048]{2,1,0:T(8,128)(2,1)} %reshape.73), calls=%async_computation.3 | async-start | bytes 4194304 | tf_op jit(solution)/shard_map/all_to_all | solution.py:110
  284.2 1.6 reshape.70
  285.8 1.6 concatenate.6
  287.4 1.9 gather_fusion.1
  289.3 1.9 gather_fusion.2
  291.1 41.4 %all-to-all-done.3 = bf16[64,7,2048]{2,1,0:T(8,128)(2,1)} async-done(((bf16[64,7,2048]{2,1,0:T(8,128)(2,1)}), bf16[64,7,2048]{2,1,0:T(8,128)(2,1)}, u32[]{:S(2)}, u32[]{:S(2)}) %all-to-all-start.3) | async-done | bytes 1835040 | tf_op jit(solution)/shard_map/all_to_all | solution.py:110
  332.5 3.8 reshape.74
  336.3 1.6 concatenate.7
  338.0 1.9 gather_fusion.4
  339.8 1.9 gather_fusion.3
  341.7 3.6 fusion.22
  345.3 0.6 pad_maximum_fusion
  345.9 19.9 %reduce-scatter.6.cloned.1.call-done = f32[1,512,768]{2,1,0:T(8,128)} async-done(((f32[1,2048,768]{2,1,0:T(8,128)}), f32[1,512,768]{2,1,0:T(8,128)}) %reduce-scatter.6.cloned.1.call-update) | async-done | bytes 1572880 | tf_op jit(solution)/shard_map/reduce_scatter | solution.py:122
  365.8 69.1 %reduce-scatter.8.cloned.1.call-done = f32[1,768,512]{2,1,0:T(8,128)} async-done(((f32[1,768,2048]{2,1,0:T(8,128)}), f32[1,768,512]{2,1,0:T(8,128)}) %reduce-scatter.8.cloned.1.call-update) | async-done | bytes 1572880 | tf_op jit(solution)/shard_map/reduce_scatter | solution.py:123
  (35 shorter events, 0.2 us)
Async XLA Ops:
  7.2 25.5 %copy-start = (bf16[160,2048]{1,0:T(8,128)(2,1)S(1)}, bf16[160,2048]{1,0:T(8,128)(2,1)}, u32[]{:S(2)}) copy-start(bf16[160,2048]{1,0:T(8,128)(2,1)} %param.9) | copy-start | bytes 1966084
  7.2 3.4 copy-start.5
  7.2 134.9 %all-gather.8.cloned.1.call-start = ((), (), s32[]{:S(2)}) async-start(), calls=%async_computation.9 | async-start | bytes 3932160 | tf_op jit(solution)/shard_map/all_gather | solution.py:55
  7.9 138.8 %all-gather.6.cloned.1.call-start = ((), (), s32[]{:S(2)}) async-start(), calls=%async_computation.8 | async-start | bytes 3932160 | tf_op jit(solution)/shard_map/all_gather | solution.py:54
  10.8 2.8 copy-start.6
  10.9 2.8 copy-start.2
  16.8 63.8 %all-to-all-start.2 = ((bf16[64,7,2048]{2,1,0:T(8,128)(2,1)}), bf16[64,7,2048]{2,1,0:T(8,128)(2,1)S(1)}, u32[]{:S(2)}, u32[]{:S(2)}) async-start(bf16[64,7,2048]{2,1,0:T(8,128)(2,1)} %reshape.71), calls=%async_computation.2 | async-start | bytes 4194304 | tf_op jit(solution)/shard_map/all_to_all | solution.py:104
  32.0 150.9 %all-gather.4.cloned.1.call-start = ((), (), s32[]{:S(2)}) async-start(), calls=%async_computation.7 | async-start | bytes 3932160 | tf_op jit(solution)/shard_map/all_gather | solution.py:53
  80.7 57.6 %all-to-all-start = ((bf16[64,7,2048]{2,1,0:T(8,128)(2,1)}), bf16[64,7,2048]{2,1,0:T(8,128)(2,1)}, u32[]{:S(2)}, u32[]{:S(2)}) async-start(bf16[64,7,2048]{2,1,0:T(8,128)(2,1)} %reshape.67), calls=%async_computation | async-start | bytes 4194304 | tf_op jit(solution)/shard_map/all_to_all | solution.py:87
  89.9 256.0 %reduce-scatter.4.cloned.1.call-start = ((), (), s32[]{:S(2)}) async-start(), calls=%async_computation.10 | async-start | bytes 7864320 | tf_op jit(solution)/shard_map/reduce_scatter | solution.py:121
  91.8 50.3 %copy-start.3 = (bf16[448,2048]{1,0:T(8,128)(2,1)S(1)}, bf16[448,2048]{1,0:T(8,128)(2,1)}, u32[]{:S(2)}) copy-start(bf16[448,2048]{1,0:T(8,128)(2,1)} %reshape.72) | copy-start | bytes 5505028
  182.8 7.4 %copy-start.4 = (bf16[448,2048]{1,0:T(8,128)(2,1)S(1)}, bf16[448,2048]{1,0:T(8,128)(2,1)}, u32[]{:S(2)}) copy-start(bf16[448,2048]{1,0:T(8,128)(2,1)} %reshape.68) | copy-start | bytes 5505028
  189.4 0.8 copy-start.8
  194.8 171.1 %reduce-scatter.6.cloned.1.call-start = ((), (), s32[]{:S(2)}) async-start(), calls=%async_computation.11 | async-start | bytes 7864320 | tf_op jit(solution)/shard_map/reduce_scatter | solution.py:122
  201.0 234.0 %reduce-scatter.8.cloned.1.call-start = ((), (), s32[]{:S(2)}) async-start(), calls=%async_computation.12 | async-start | bytes 7864320 | tf_op jit(solution)/shard_map/reduce_scatter | solution.py:123
  212.6 64.2 %all-to-all-start.1 = ((bf16[64,7,2048]{2,1,0:T(8,128)(2,1)}), bf16[64,7,2048]{2,1,0:T(8,128)(2,1)S(1)}, u32[]{:S(2)}, u32[]{:S(2)}) async-start(bf16[64,7,2048]{2,1,0:T(8,128)(2,1)} %reshape.69), calls=%async_computation.1 | async-start | bytes 4194304 | tf_op jit(solution)/shard_map/all_to_all | solution.py:92
  225.5 3.9 copy-start.7
  225.5 3.9 copy-start.9
  276.7 55.8 %all-to-all-start.3 = ((bf16[64,7,2048]{2,1,0:T(8,128)(2,1)}), bf16[64,7,2048]{2,1,0:T(8,128)(2,1)}, u32[]{:S(2)}, u32[]{:S(2)}) async-start(bf16[64,7,2048]{2,1,0:T(8,128)(2,1)} %reshape.73), calls=%async_computation.3 | async-start | bytes 4194304 | tf_op jit(solution)/shard_map/all_to_all | solution.py:110
  339.8 95.1 %copy-start.1 = (bf16[160,2048]{1,0:T(8,128)(2,1)S(1)}, bf16[160,2048]{1,0:T(8,128)(2,1)}, u32[]{:S(2)}) copy-start(bf16[160,2048]{1,0:T(8,128)(2,1)} %param.9) | copy-start | bytes 1966084
Sparse Core Ops, SparseCore 0:
  9.8 65.1 all-gather.7
  76.8 62.9 all-gather.5
  141.6 41.1 all-gather.3
  194.9 88.2 reduce-scatter.3
  286.1 79.6 reduce-scatter.5
  368.8 66.0 reduce-scatter.7
where the time goes:
time: 443 us; the launch traced here: 442 us
  waiting for transfers between devices  293 us (66%)
  matrix products  46.9 us (11%)
  starting transfers between devices  45.1 us (10%)
  local copies, waits for them, and re-layouts  36.3 us (8%)
  between operations  14.4 us (3%)
  other arithmetic  5.72 us (1%)
    reduce_scatter x1, waiting for transfers between devices, on_device(): lax.psum_scatter(part_down, 'dp', scatter_dimension=2, tiled=True)  69.1 us
    all_to_all x1, waiting for transfers between devices, on_device(): lax.all_to_all(x_slots, 'expert', split_axis=0, concat_axis=0, tiled=True)  46.6 us
    all_to_all x1, waiting for transfers between devices, on_device(): lax.all_to_all(g_slots, 'expert', split_axis=0, concat_axis=0, tiled=True)  42.5 us
    all_to_all x1, waiting for transfers between devices, on_device(): lax.all_to_all(d_rows.reshape(experts, capacity, model_width), 'expert',...  41.4 us
    all_to_all x1, waiting for transfers between devices, on_device(): lax.all_to_all(result.reshape(item_shape), 'expert', split_axis=0, concat...  40.8 us
    all_gather x1, waiting for transfers between devices, on_device(): lax.all_gather(w_gate, 'dp', axis=1, tiled=True)  31 us
    reduce_scatter x1, waiting for transfers between devices, on_device(): lax.psum_scatter(part_up, 'dp', scatter_dimension=1, tiled=True)  19.9 us
    dot_general x3, matrix products, contract_rows(): lax.dot_general(first_op, second_op, (((0,), (0,)), ((), ())), preferred_...  16.1 us
  transfers between devices with their start and end apart: 10, of which 7 were waited for; matrix products, arithmetic and copies ran while one was open for 17% of the time, Pallas kernels for 0%

commit v1 on v0

v1 whole, which is shorter than its diff:
```python
import functools

import jax
import jax.numpy as jnp
from jax import lax
from jax.experimental import pallas as pl
from jax.experimental.pallas import tpu as pltpu
from jax.sharding import PartitionSpec as P

MESH = pl.DeviceIdType.MESH
LANE = 128
PLANE = 8
NY = 4
TILE = 256
F32 = jnp.float32
BF16 = jnp.bfloat16


def mm(a, b):
    return jnp.dot(a, b, preferred_element_type=F32)


def mm_last(a, b):
    return lax.dot_general(a, b, (((1,), (1,)), ((), ())), preferred_element_type=F32)


def mm_first(a, b):
    return lax.dot_general(a, b, (((0,), (0,)), ((), ())), preferred_element_type=F32)


def kernel(
    cap,
    tok, routes, probs, cot, wg_in, wu_in, wd_in,
    lay_o, dtok_o, dgate_o, gg_o, gu_o, gd_o,
    slot_s, rg, xs, gs, os_, xr, gr, orr, dxr, X, XT, HT, WG, WU, WD, A, B, HID, DG, DU, scr,
    sib_s, sib_r, sibd_s, sibd_r, crs_s, crs_r, crsd_s, crsd_r, fin, find,
    a2a_send, a2a_recv, a2a_loc, ag_loc, ag_send, ag_cross, ag_sib, ag_fwd_s, ag_fwd_r,
    sib_ss, sib_rs, crs_ss, crs_rs, out_sem,
):
    T, D = tok.shape
    E = lax.axis_size("expert")
    NZ = E // PLANE
    S = E * cap
    ROWS = D // LANE
    NP = WG.shape[0]
    PC = D // NP
    FF = WG.shape[2]
    CH = PLANE * cap
    dp = lax.axis_index("dp")
    me = lax.axis_index("expert")
    core, xlo = dp % 2, dp // 2
    sib_dp = 2 * xlo + (1 - core)
    crs_dp = 2 * (1 - xlo) + core
    sibling, across = (sib_dp, me), (crs_dp, me)
    my_z, my_y, my_x = me // PLANE, (me // 2) % NY, me % 2

    def partner(dz, i):
        dy, dx = i // 2, i % 2
        e = ((my_z + dz) % NZ) * PLANE + ((my_y + dy) % NY) * 2 + (my_x + dx) % 2
        return (dp + 2 * dx) % 4, e

    barrier = pltpu.get_barrier_semaphore()

    def greet(k, carry):
        pl.semaphore_signal(barrier, inc=1, device_id=partner(k // PLANE, k % PLANE), device_id_type=MESH)
        return carry

    lax.fori_loop(1, E, greet, 0)
    pl.semaphore_signal(barrier, inc=1, device_id=sibling, device_id_type=MESH)
    pl.semaphore_signal(barrier, inc=1, device_id=across, device_id_type=MESH)

    r0, r1 = routes[:, 0:1], routes[:, 1:2]
    iota_e = lax.broadcasted_iota(jnp.int32, (T, E), 1)
    h0, h1 = r0 == iota_e, r1 == iota_e
    hits = (jnp.where(h0, 1.0, 0.0) + jnp.where(h1, 1.0, 0.0)).astype(BF16)
    tri = jnp.where(
        lax.broadcasted_iota(jnp.int32, (T, T), 0) > lax.broadcasted_iota(jnp.int32, (T, T), 1), 1.0, 0.0
    ).astype(BF16)
    before = mm(tri, hits)
    for k, (r, h) in enumerate(((r0, h0), (r1, h1))):
        rank = jnp.sum(jnp.where(h, before, 0.0), axis=1, keepdims=True).astype(jnp.int32)
        slot_s[:, k : k + 1] = jnp.where(rank < cap, r * cap + rank, S)
        rg[k * T : (k + 1) * T, :] = (probs[:, k : k + 1] * cot[...].astype(F32)).astype(BF16)

    pl.semaphore_wait(barrier, E + 1)

    mats = ((wg_in, WG), (wu_in, WU), (wd_in, WD))
    ag = []
    for m, (src, full) in enumerate(mats):
        c = pltpu.make_async_remote_copy(
            src, full.at[dp], ag_send.at[m], ag_cross.at[m], device_id=across, device_id_type=MESH
        )
        c.start()
        s = pltpu.make_async_remote_copy(
            src, full.at[dp], ag_send.at[3 + m], ag_sib.at[m], device_id=sibling, device_id_type=MESH
        )
        s.start()
        l = pltpu.make_async_copy(src, full.at[dp], ag_loc.at[m])
        l.start()
        ag.append((c, s, l))

    def send_block(a, src, dst, dz, i):
        d, e = partner(dz, i)
        pltpu.make_async_remote_copy(
            src.at[pl.ds(e * cap, cap)],
            dst.at[pl.ds(me * cap, cap)],
            a2a_send.at[a],
            a2a_recv.at[a],
            device_id=(d, e),
            device_id_type=MESH,
        ).start()

    def exchange(a, fill, src, dst):
        def plane(q, carry):
            half = (q + 1) // 2
            dz = (NZ // 2 + half * (2 * (q % 2) - 1)) % NZ
            fill(((my_z + dz) % NZ) * CH)

            def one(i, c):
                send_block(a, src, dst, dz, i)
                return c

            lax.fori_loop(0, PLANE, one, 0)
            return carry

        lax.fori_loop(0, NZ - 1, plane, 0)
        fill(my_z * CH)
        mine = pl.ds(me * cap, cap)
        pltpu.make_async_copy(src.at[mine], dst.at[mine], a2a_loc.at[a]).start()

        def rest(i, c):
            send_block(a, src, dst, 0, i)
            return c

        lax.fori_loop(1, PLANE, rest, 0)

    def arrived(a, src, dst):
        block = dst.at[pl.ds(0, S - cap)]
        pltpu.make_async_copy(block, block, a2a_recv.at[a]).wait()
        mine = pl.ds(me * cap, cap)
        pltpu.make_async_copy(src.at[mine], dst.at[mine], a2a_loc.at[a]).wait()

    def sent(a, src):
        block = src.at[pl.ds(0, S - cap)]
        pltpu.make_async_copy(block, block, a2a_send.at[a]).wait()

    def lay_rows(v, dst, base):
        for j in range(ROWS):
            scr[pl.ds(j, CH, stride=ROWS), :] = v[:, j * LANE : (j + 1) * LANE]
        dst[pl.ds(base, CH)] = scr[pl.ds(0, CH * ROWS), :].reshape(CH, ROWS, LANE).astype(BF16)

    def onehot(k, base, n):
        return jnp.where(
            slot_s[:, k : k + 1] == lax.broadcasted_iota(jnp.int32, (T, n), 1) + base, 1.0, 0.0
        )

    def fill_x(base):
        pick = (onehot(0, base, CH) + onehot(1, base, CH)).astype(BF16)
        lay_rows(mm_first(pick, tok[...]), xs, base)

    def fill_g(base):
        v = mm_first(onehot(0, base, CH).astype(BF16), rg[0:T, :])
        v += mm_first(onehot(1, base, CH).astype(BF16), rg[T : 2 * T, :])
        lay_rows(v, gs, base)

    exchange(0, fill_x, xs, xr)
    exchange(1, fill_g, gs, gr)

    def forward_weights(m):
        full = mats[m][1]
        ag[m][0].wait_recv()
        f = pltpu.make_async_remote_copy(
            full.at[crs_dp], full.at[crs_dp], ag_fwd_s.at[m], ag_fwd_r.at[m], device_id=sibling, device_id_type=MESH
        )
        f.start()
        return f

    def weights_here(m, f):
        ag[m][2].wait()
        ag[m][1].wait_recv()
        f.wait_recv()

    def unpack(src):
        step = 16 * cap

        def chunk(c, carry):
            rows = pl.ds(pl.multiple_of(c * step, 16), step)
            scr[pl.ds(0, step * ROWS), :] = src[rows].astype(F32).reshape(step * ROWS, LANE)
            for j in range(ROWS):
                p, o = divmod(j * LANE, PC)
                X[p, rows, o : o + LANE] = scr[pl.ds(j, step, stride=ROWS), :].astype(BF16)
            return carry

        lax.fori_loop(0, S // step, chunk, 0)

    fwd = [forward_weights(0), forward_weights(1)]
    arrived(0, xs, xr)
    unpack(xr)
    weights_here(0, fwd[0])
    weights_here(1, fwd[1])

    def up_tile(n, carry):
        cols = pl.ds(pl.multiple_of(n * TILE, TILE), TILE)
        gate = mm(X[0], WG[0, :, cols])
        up = mm(X[0], WU[0, :, cols])
        for p in range(1, NP):
            gate += mm(X[p], WG[p, :, cols])
            up += mm(X[p], WU[p, :, cols])
        s = jax.nn.sigmoid(gate)
        act = gate * s
        A[:, cols] = up * (s * (1.0 + gate * (1.0 - s)))
        B[:, cols] = act
        HID[:, cols] = (act * up).astype(BF16)
        return carry

    lax.fori_loop(0, FF // TILE, up_tile, 0)
    fwd.append(forward_weights(2))
    weights_here(2, fwd[2])

    def rows_out(p, v):
        for j in range(PC // LANE):
            scr[pl.ds(p * (PC // LANE) + j, S, stride=ROWS), :] = v[:, j * LANE : (j + 1) * LANE]

    def fill_from_scr(dst):
        def fill(base):
            dst[pl.ds(base, CH)] = (
                scr[pl.ds(pl.multiple_of(base * ROWS, ROWS), CH * ROWS), :].reshape(CH, ROWS, LANE).astype(BF16)
            )

        return fill

    for p in range(NP):
        rows_out(p, mm(HID[...], WD[p]))
    exchange(2, fill_from_scr(os_), os_, orr)

    for p in range(NP):
        XT[p] = X[p].T
    HT[...] = HID[...].T

    arrived(1, gs, gr)
    unpack(gr)

    def to_sibling(k, buf_s, buf_r, s):
        c = pltpu.make_async_remote_copy(
            buf_s, buf_r, sib_ss.at[k, s], sib_rs.at[k, s], device_id=sibling, device_id_type=MESH
        )
        c.start()
        return c

    def to_across(k, buf_s, buf_r):
        c = pltpu.make_async_remote_copy(
            buf_s, buf_r, crs_ss.at[k], crs_rs.at[k], device_id=across, device_id_type=MESH
        )
        c.start()
        return c

    def part_down(p):
        return mm(HT[...], X[p])

    def part_gu(m, p):
        return mm(XT[p], (DG, DU)[m][...])

    sib = {}
    for s in range(2):
        sibd_s[s] = part_down(2 * s + (1 - core)).astype(BF16)
        sib[2, s] = to_sibling(2, sibd_s.at[s], sibd_r.at[s], s)

    def dh_tile(n, carry):
        cols = pl.ds(pl.multiple_of(n * TILE, TILE), TILE)
        dh = mm_last(X[0], WD[0, cols, :])
        for p in range(1, NP):
            dh += mm_last(X[p], WD[p, cols, :])
        DG[:, cols] = (dh * A[:, cols]).astype(BF16)
        DU[:, cols] = (dh * B[:, cols]).astype(BF16)
        return carry

    lax.fori_loop(0, FF // TILE, dh_tile, 0)
    for m in range(2):
        for s in range(2):
            sib_s[m, s] = part_gu(m, 2 * s + (1 - core)).astype(BF16)
            sib[m, s] = to_sibling(m, sib_s.at[m, s], sib_r.at[m, s], s)

    for s in range(2):
        sib[2, s].wait_recv()
    crsd_s[...] = (part_down(crs_dp) + sibd_r[1 - xlo].astype(F32)).astype(BF16)
    crs = [None, None, to_across(2, crsd_s, crsd_r)]
    for m in range(2):
        for s in range(2):
            sib[m, s].wait_recv()
        crs_s[m] = (part_gu(m, crs_dp) + sib_r[m, 1 - xlo].astype(F32)).astype(BF16)
        crs[m] = to_across(m, crs_s.at[m], crs_r.at[m])

    sent(0, xs)
    for p in range(NP):
        rows_out(p, mm_last(DG[...], WG[p]) + mm_last(DU[...], WU[p]))
    exchange(3, fill_from_scr(xs), xs, dxr)

    find[...] = part_down(dp) + sibd_r[xlo].astype(F32)
    for m in range(2):
        fin[m] = part_gu(m, dp) + sib_r[m, xlo].astype(F32)

    arrived(2, os_, orr)
    unpack(orr)
    p0, p1 = onehot(0, 0, S).astype(BF16), onehot(1, 0, S).astype(BF16)
    dg0 = jnp.zeros((T, 1), F32)
    dg1 = jnp.zeros((T, 1), F32)
    for p in range(NP):
        cols = slice(p * PC, (p + 1) * PC)
        k0, k1 = mm(p0, X[p]), mm(p1, X[p])
        lay_o[:, cols] = (probs[:, 0:1] * k0 + probs[:, 1:2] * k1).astype(BF16)
        c32 = cot[:, cols].astype(F32)
        dg0 += jnp.sum(c32 * k0, axis=1, keepdims=True)
        dg1 += jnp.sum(c32 * k1, axis=1, keepdims=True)
    dgate_o[:, 0:1] = dg0
    dgate_o[:, 1:2] = dg1

    outs = []
    crs[2].wait_recv()
    find[...] += crsd_r[...].astype(F32)
    outs.append(pltpu.make_async_copy(find, gd_o, out_sem.at[2]))
    outs[-1].start()
    for m, o in enumerate((gg_o, gu_o)):
        crs[m].wait_recv()
        fin[m] += crs_r[m].astype(F32)
        outs.append(pltpu.make_async_copy(fin.at[m], o, out_sem.at[m]))
        outs[-1].start()

    arrived(3, xs, dxr)
    unpack(dxr)
    both = p0 + p1
    for p in range(NP):
        dtok_o[:, p * PC : (p + 1) * PC] = mm(both, X[p]).astype(BF16)

    sent(1, gs)
    sent(2, os_)
    sent(3, xs)
    for m in range(3):
        ag[m][0].wait_send()
        ag[m][1].wait_send()
        fwd[m].wait_send()
        crs[m].wait_send()
        for s in range(2):
            sib[m, s].wait_send()
    for o in outs:
        o.wait()


def on_device(tokens, routes, gate_probs, cotangent, w_gate, w_up, w_down):
    T, D = tokens.shape
    E = lax.axis_size("expert")
    NP = lax.axis_size("dp")
    PC, FF = w_gate.shape[1:]
    cap = max(2, 3 * T * routes.shape[1] // (2 * E))
    S = E * cap
    ROWS = D // LANE
    slots = pltpu.VMEM((S, ROWS, LANE), BF16)
    dma = pltpu.SemaphoreType.DMA
    vmem = pl.BlockSpec(memory_space=pltpu.VMEM)
    hbm = pl.BlockSpec(memory_space=pl.ANY)
    scratch = [
        pltpu.VMEM((T, 2), jnp.int32),
        pltpu.VMEM((2 * T, D), BF16),
        *([slots] * 7),
        pltpu.VMEM((NP, S, PC), BF16),
        pltpu.VMEM((NP, PC, S), BF16),
        pltpu.VMEM((FF, S), BF16),
        pltpu.VMEM((NP, PC, FF), BF16),
        pltpu.VMEM((NP, PC, FF), BF16),
        pltpu.VMEM((NP, FF, PC), BF16),
        pltpu.VMEM((S, FF), F32),
        pltpu.VMEM((S, FF), F32),
        *([pltpu.VMEM((S, FF), BF16)] * 3),
        pltpu.VMEM((S * ROWS, LANE), F32),
        pltpu.VMEM((2, 2, PC, FF), BF16),
        pltpu.VMEM((2, 2, PC, FF), BF16),
        pltpu.VMEM((2, FF, PC), BF16),
        pltpu.VMEM((2, FF, PC), BF16),
        pltpu.VMEM((2, PC, FF), BF16),
        pltpu.VMEM((2, PC, FF), BF16),
        pltpu.VMEM((FF, PC), BF16),
        pltpu.VMEM((FF, PC), BF16),
        pltpu.VMEM((2, PC, FF), F32),
        pltpu.VMEM((FF, PC), F32),
        dma((4,)), dma((4,)), dma((4,)),
        dma((3,)), dma((6,)), dma((3,)), dma((3,)), dma((3,)), dma((3,)),
        dma((3, 2)), dma((3, 2)), dma((3,)), dma((3,)), dma((3,)),
    ]
    lay, dtok, dgates, gg, gu, gd = pl.pallas_call(
        functools.partial(kernel, cap),
        out_shape=(
            jax.ShapeDtypeStruct((T, D), BF16),
            jax.ShapeDtypeStruct((T, D), BF16),
            jax.ShapeDtypeStruct((T, 2), F32),
            jax.ShapeDtypeStruct((PC, FF), F32),
            jax.ShapeDtypeStruct((PC, FF), F32),
            jax.ShapeDtypeStruct((FF, PC), F32),
        ),
        in_specs=[vmem, vmem, vmem, vmem, hbm, hbm, hbm],
        out_specs=(vmem, vmem, vmem, hbm, hbm, hbm),
        scratch_shapes=scratch,
        compiler_params=pltpu.CompilerParams(
            collective_id=0, has_side_effects=True, vmem_limit_bytes=64000 * 1024
        ),
    )(tokens, routes, gate_probs, cotangent, w_gate[0], w_up[0], w_down[0])
    return lay, dtok, dgates, gg[None], gu[None], gd[None]


def solution(mesh):
    rows = P(("dp", "expert"), None)
    weights = (P("expert", "dp", None), P("expert", "dp", None), P("expert", None, "dp"))
    return jax.shard_map(
        on_device,
        mesh=mesh,
        in_specs=(rows, rows, rows, rows, *weights),
        out_specs=(rows, rows, rows, *weights),
        check_vma=False,
    )
```

time: 443 us -> 194 us (0.44)
  waiting for transfers between devices: 293 us -> 0 us
  Pallas kernels: 0 us -> 180 us
  matrix products: 46.9 us -> 0 us
  starting transfers between devices: 45.1 us -> 0 us
  local copies, waits for them, and re-layouts: 36.3 us -> 13.6 us
  between operations: 14.4 us -> 0.65 us
  other arithmetic: 5.72 us -> 0 us
    pallas_call x0 -> x1, Pallas kernels: none -> 180 us  [on_device(): pl.pallas_call(functools.partial(kernel, cap), out_shape=(jax.ShapeDtypeS...]
    all_to_all x4 -> x0, waiting for transfers between devices: 171 us -> none  [the longest x1 46.6 us: on_device(): lax.all_to_all(x_slots, 'expert', split_axis=0, concat_axis=0, tiled=True)]
    reduce_scatter x3 -> x0, waiting for transfers between devices: 89 us -> none  [the longest x1 69.1 us: on_device(): lax.psum_scatter(part_down, 'dp', scatter_dimension=2, tiled=True)]
    dot_general x12 -> x0, matrix products: 46.9 us -> none  [the longest x3 16.1 us: contract_rows(): lax.dot_general(first_op, second_op, (((0,), (0,)), ((), ())), preferred_...]
    all_to_all x4 -> x0, starting transfers between devices: 44.6 us -> none  [the longest x1 15.1 us: on_device(): lax.all_to_all(g_slots, 'expert', split_axis=0, concat_axis=0, tiled=True)]
    all_gather x3 -> x0, waiting for transfers between devices: 31 us -> none  [the longest x1 31 us: on_device(): lax.all_gather(w_gate, 'dp', axis=1, tiled=True)]
    reshape x8 -> x0, local copies, waits for them, and re-layouts: 21.3 us -> none  [the longest x1 3.78 us: on_device(): dx_pad = jnp.concatenate([dx_back.reshape(-1, model_width), zero_row], 0)]
    unnamed x20 -> x14, local copies, waits for them, and re-layouts: 0.89 us -> 13.6 us
  transfers between devices with their start and end apart: 10 -> 0, of which waited for: 7 -> 0; matrix products, arithmetic and copies ran while one was open for 17% -> 0% of each run, Pallas kernels for 0% -> 0%
where the time goes in v1:
time: 194 us
  Pallas kernels  180 us (93%)
  local copies, waits for them, and re-layouts  13.6 us (7%)
    pallas_call x1, Pallas kernels, on_device(): pl.pallas_call(functools.partial(kernel, cap), out_shape=(jax.ShapeDtypeS...  180 us
    unnamed x14, local copies, waits for them, and re-layouts  13.6 us

profile of v1, /device:TPU:1, one launch (start us, length us, event | category | flops | bytes accessed | tf_op | source)
XLA Modules:
  0.0 193.8 jit_solution(11224620963162557449)
XLA Ops:
  0.6 1.4 copy.13.routes
  2.1 1.4 copy.14.probs
  3.5 179.6 %shard_map.118 = (bf16[160,2048]{1,0:T(8,128)(2,1)}, bf16[160,2048]{1,0:T(8,128)(2,1)}, f32[160,2]{1,0:T(8,128)}, f32[512,768]{1,0:T(8,128)}, f32[512,768]{1,0:T(8,128)}, /*index=5*/f32[768,512]{1,0:T(8,128)}) custom-call(bf16[160,2048]{1,0:T(8,128)(2,1)} %tok.1, s32[160,2]{1,0:T(8,128)} %copy.13.routes, f32[160,2]{1,0:T(8,128)} %copy.14.probs, ...), custom_call_target="tpu_custom_call" | custom-call | tf_op jit(solution)/shard_map/pallas_call | solution.py:388
  183.1 0.0 copy-start.2
  183.1 1.7 copy.15
  184.8 2.0 %copy.21 = bf16[160,2048]{1,0:T(8,128)(2,1)} copy(bf16[160,2048]{1,0:T(8,128)(2,1)} %get-tuple-element.30) | data formatting | bytes 1310720
  186.8 2.0 %copy.22 = bf16[160,2048]{1,0:T(8,128)(2,1)} copy(bf16[160,2048]{1,0:T(8,128)(2,1)} %get-tuple-element.31) | data formatting | bytes 1310720
  188.7 0.0 copy-done.2
  188.7 0.0 copy-start.1
  188.7 1.1 copy.23
  189.9 0.8 copy-done.1
  190.7 0.0 copy-start
  190.7 1.1 copy.24
  191.9 0.8 copy-done
  192.7 1.1 copy.25
Async XLA Ops:
  183.1 5.6 %copy-start.2 = (f32[512,768]{1,0:T(8,128)S(1)}, f32[512,768]{1,0:T(8,128)}, u32[]{:S(2)}) copy-start(f32[512,768]{1,0:T(8,128)} %get-tuple-element.15) | copy-start | bytes 4718596
  188.7 2.0 %copy-start.1 = (f32[512,768]{1,0:T(8,128)S(1)}, f32[512,768]{1,0:T(8,128)}, u32[]{:S(2)}) copy-start(f32[512,768]{1,0:T(8,128)} %get-tuple-element.16) | copy-start | bytes 4718596
  190.7 2.0 %copy-start = (f32[768,512]{1,0:T(8,128)S(1)}, f32[768,512]{1,0:T(8,128)}, u32[]{:S(2)}) copy-start(f32[768,512]{1,0:T(8,128)} %get-tuple-element.17) | copy-start | bytes 4718596

commit v2 on v1

--- a/solution.py
+++ b/solution.py
@@ -30,12 +30,12 @@
 
 def kernel(
     cap,
-    tok, routes, probs, cot, wg_in, wu_in, wd_in,
-    lay_o, dtok_o, dgate_o, gg_o, gu_o, gd_o,
-    slot_s, rg, xs, gs, os_, xr, gr, orr, dxr, X, XT, HT, WG, WU, WD, A, B, HID, DG, DU, scr,
+    tok_in, routes_in, probs_in, cot_in, wg_in, wu_in, wd_in,
+    lay_o, dgate_o, slot_o, dxr, gg_o, gu_o, gd_o,
+    tok, routes, probs_t, cot, probs, lay, dgate, slot_s, rg, xs, gs, os_, xr, gr, orr, X, XT, HT, WG, WU, WD, A, B, HID, DG, DU, scr,
     sib_s, sib_r, sibd_s, sibd_r, crs_s, crs_r, crsd_s, crsd_r, fin, find,
     a2a_send, a2a_recv, a2a_loc, ag_loc, ag_send, ag_cross, ag_sib, ag_fwd_s, ag_fwd_r,
-    sib_ss, sib_rs, crs_ss, crs_rs, out_sem,
+    sib_ss, sib_rs, crs_ss, crs_rs, in_sem, out_sem,
 ):
     T, D = tok.shape
     E = lax.axis_size("expert")
@@ -48,28 +48,39 @@
     CH = PLANE * cap
     dp = lax.axis_index("dp")
     me = lax.axis_index("expert")
-    core, xlo = dp % 2, dp // 2
+    core, xlo = lax.rem(dp, 2), lax.div(dp, 2)
     sib_dp = 2 * xlo + (1 - core)
     crs_dp = 2 * (1 - xlo) + core
     sibling, across = (sib_dp, me), (crs_dp, me)
-    my_z, my_y, my_x = me // PLANE, (me // 2) % NY, me % 2
+    my_z, my_y, my_x = lax.div(me, PLANE), lax.rem(lax.div(me, 2), NY), lax.rem(me, 2)
 
     def partner(dz, i):
-        dy, dx = i // 2, i % 2
-        e = ((my_z + dz) % NZ) * PLANE + ((my_y + dy) % NY) * 2 + (my_x + dx) % 2
-        return (dp + 2 * dx) % 4, e
+        dy, dx = lax.div(i, 2), lax.rem(i, 2)
+        e = lax.rem(my_z + dz, NZ) * PLANE + lax.rem(my_y + dy, NY) * 2 + lax.rem(my_x + dx, 2)
+        return lax.rem(dp + 2 * dx, 4), e
 
     barrier = pltpu.get_barrier_semaphore()
 
     def greet(k, carry):
-        pl.semaphore_signal(barrier, inc=1, device_id=partner(k // PLANE, k % PLANE), device_id_type=MESH)
+        pl.semaphore_signal(barrier, inc=1, device_id=partner(lax.div(k, PLANE), lax.rem(k, PLANE)), device_id_type=MESH)
         return carry
 
     lax.fori_loop(1, E, greet, 0)
     pl.semaphore_signal(barrier, inc=1, device_id=sibling, device_id_type=MESH)
     pl.semaphore_signal(barrier, inc=1, device_id=across, device_id_type=MESH)
 
-    r0, r1 = routes[:, 0:1], routes[:, 1:2]
+    ins = []
+    for i, (src, dst) in enumerate(((routes_in, routes), (probs_in, probs_t), (tok_in, tok), (cot_in, cot))):
+        ins.append(pltpu.make_async_copy(src, dst, in_sem.at[i]))
+        ins[-1].start()
+
+    eye = lax.broadcasted_iota(jnp.int32, (T, T), 0) == lax.broadcasted_iota(jnp.int32, (T, T), 1)
+
+    def column(row):
+        return jnp.sum(jnp.where(eye, row, jnp.zeros_like(row)), axis=1, keepdims=True)
+
+    ins[0].wait()
+    r0, r1 = column(routes[0:1, :]), column(routes[1:2, :])
     iota_e = lax.broadcasted_iota(jnp.int32, (T, E), 1)
     h0, h1 = r0 == iota_e, r1 == iota_e
     hits = (jnp.where(h0, 1.0, 0.0) + jnp.where(h1, 1.0, 0.0)).astype(BF16)
@@ -80,10 +91,79 @@
     for k, (r, h) in enumerate(((r0, h0), (r1, h1))):
         rank = jnp.sum(jnp.where(h, before, 0.0), axis=1, keepdims=True).astype(jnp.int32)
         slot_s[:, k : k + 1] = jnp.where(rank < cap, r * cap + rank, S)
-        rg[k * T : (k + 1) * T, :] = (probs[:, k : k + 1] * cot[...].astype(F32)).astype(BF16)
-
+
+    def send_block(a, src, dst, dz, i):
+        d, e = partner(dz, i)
+        pltpu.make_async_remote_copy(
+            src.at[pl.ds(e * cap, cap)],
+            dst.at[pl.ds(me * cap, cap)],
+            a2a_send.at[a],
+            a2a_recv.at[a],
+            device_id=(d, e),
+            device_id_type=MESH,
+        ).start()
+
+    def exchange(a, fill, src, dst, filled=False):
+        def send_plane(dz):
+            def one(i, c):
+                send_block(a, src, dst, dz, i)
+                return c
+
+            lax.fori_loop(0, PLANE, one, 0)
+
+        def plane(q, carry):
+            half = lax.div(q + 1, 2)
+            dz = lax.rem(NZ // 2 + half * (2 * lax.rem(q, 2) - 1), NZ)
+            fill(lax.rem(my_z + dz, NZ) * CH)
+            send_plane(dz)
+            return carry
+
+        if filled:
+            send_plane(NZ // 2)
+        lax.fori_loop(1 if filled else 0, NZ - 1, plane, 0)
+        fill(my_z * CH)
+        mine = pl.ds(me * cap, cap)
+        pltpu.make_async_copy(src.at[mine], dst.at[mine], a2a_loc.at[a]).start()
+
+        def rest(i, c):
+            send_block(a, src, dst, 0, i)
+            return c
+
+        lax.fori_loop(1, PLANE, rest, 0)
+
+    def arrived(a, src, dst):
+        block = dst.at[pl.ds(0, S - cap)]
+        pltpu.make_async_copy(block, block, a2a_recv.at[a]).wait()
+        mine = pl.ds(me * cap, cap)
+        pltpu.make_async_copy(src.at[mine], dst.at[mine], a2a_loc.at[a]).wait()
+
+    def sent(a, src):
+        block = src.at[pl.ds(0, S - cap)]
+        pltpu.make_async_copy(block, block, a2a_send.at[a]).wait()
+
+    def lay_rows(v, dst, base):
+        for j in range(ROWS):
+            scr[pl.ds(j, CH, stride=ROWS), :] = v[:, j * LANE : (j + 1) * LANE]
+        dst[pl.ds(base, CH)] = scr[pl.ds(0, CH * ROWS), :].reshape(CH, ROWS, LANE).astype(BF16)
+
+    def onehot(k, base, n):
+        return jnp.where(
+            slot_s[:, k : k + 1] == lax.broadcasted_iota(jnp.int32, (T, n), 1) + base, 1.0, 0.0
+        )
+
+    def fill_x(base):
+        pick = (onehot(0, base, CH) + onehot(1, base, CH)).astype(BF16)
+        lay_rows(mm_first(pick, tok[...]), xs, base)
+
+    def fill_g(base):
+        v = mm_first(onehot(0, base, CH).astype(BF16), rg[0:T, :])
+        v += mm_first(onehot(1, base, CH).astype(BF16), rg[T : 2 * T, :])
+        lay_rows(v, gs, base)
+
+    first = lax.rem(my_z + NZ // 2, NZ) * CH
+    ins[2].wait()
+    fill_x(first)
     pl.semaphore_wait(barrier, E + 1)
-
     mats = ((wg_in, WG), (wu_in, WU), (wd_in, WD))
     ag = []
     for m, (src, full) in enumerate(mats):
@@ -99,71 +179,12 @@
         l.start()
         ag.append((c, s, l))
 
-    def send_block(a, src, dst, dz, i):
-        d, e = partner(dz, i)
-        pltpu.make_async_remote_copy(
-            src.at[pl.ds(e * cap, cap)],
-            dst.at[pl.ds(me * cap, cap)],
-            a2a_send.at[a],
-            a2a_recv.at[a],
-            device_id=(d, e),
-            device_id_type=MESH,
-        ).start()
-
-    def exchange(a, fill, src, dst):
-        def plane(q, carry):
-            half = (q + 1) // 2
-            dz = (NZ // 2 + half * (2 * (q % 2) - 1)) % NZ
-            fill(((my_z + dz) % NZ) * CH)
-
-            def one(i, c):
-                send_block(a, src, dst, dz, i)
-                return c
-
-            lax.fori_loop(0, PLANE, one, 0)
-            return carry
-
-        lax.fori_loop(0, NZ - 1, plane, 0)
-        fill(my_z * CH)
-        mine = pl.ds(me * cap, cap)
-        pltpu.make_async_copy(src.at[mine], dst.at[mine], a2a_loc.at[a]).start()
-
-        def rest(i, c):
-            send_block(a, src, dst, 0, i)
-            return c
-
-        lax.fori_loop(1, PLANE, rest, 0)
-
-    def arrived(a, src, dst):
-        block = dst.at[pl.ds(0, S - cap)]
-        pltpu.make_async_copy(block, block, a2a_recv.at[a]).wait()
-        mine = pl.ds(me * cap, cap)
-        pltpu.make_async_copy(src.at[mine], dst.at[mine], a2a_loc.at[a]).wait()
-
-    def sent(a, src):
-        block = src.at[pl.ds(0, S - cap)]
-        pltpu.make_async_copy(block, block, a2a_send.at[a]).wait()
-
-    def lay_rows(v, dst, base):
-        for j in range(ROWS):
-            scr[pl.ds(j, CH, stride=ROWS), :] = v[:, j * LANE : (j + 1) * LANE]
-        dst[pl.ds(base, CH)] = scr[pl.ds(0, CH * ROWS), :].reshape(CH, ROWS, LANE).astype(BF16)
-
-    def onehot(k, base, n):
-        return jnp.where(
-            slot_s[:, k : k + 1] == lax.broadcasted_iota(jnp.int32, (T, n), 1) + base, 1.0, 0.0
-        )
-
-    def fill_x(base):
-        pick = (onehot(0, base, CH) + onehot(1, base, CH)).astype(BF16)
-        lay_rows(mm_first(pick, tok[...]), xs, base)
-
-    def fill_g(base):
-        v = mm_first(onehot(0, base, CH).astype(BF16), rg[0:T, :])
-        v += mm_first(onehot(1, base, CH).astype(BF16), rg[T : 2 * T, :])
-        lay_rows(v, gs, base)
-
-    exchange(0, fill_x, xs, xr)
+    exchange(0, fill_x, xs, xr, True)
+    ins[1].wait()
+    ins[3].wait()
+    for k in range(2):
+        probs[:, k : k + 1] = column(probs_t[k : k + 1, :])
+        rg[k * T : (k + 1) * T, :] = (probs[:, k : k + 1] * cot[...].astype(F32)).astype(BF16)
     exchange(1, fill_g, gs, gr)
 
     def forward_weights(m):
@@ -307,14 +328,17 @@
     for p in range(NP):
         cols = slice(p * PC, (p + 1) * PC)
         k0, k1 = mm(p0, X[p]), mm(p1, X[p])
-        lay_o[:, cols] = (probs[:, 0:1] * k0 + probs[:, 1:2] * k1).astype(BF16)
+        lay[:, cols] = (probs[:, 0:1] * k0 + probs[:, 1:2] * k1).astype(BF16)
         c32 = cot[:, cols].astype(F32)
         dg0 += jnp.sum(c32 * k0, axis=1, keepdims=True)
         dg1 += jnp.sum(c32 * k1, axis=1, keepdims=True)
-    dgate_o[:, 0:1] = dg0
-    dgate_o[:, 1:2] = dg1
+    for k, v in enumerate((dg0, dg1)):
+        dgate[k : k + 1, :] = jnp.sum(jnp.where(eye, v, 0.0), axis=0, keepdims=True)
 
     outs = []
+    for i, (src, dst) in enumerate(((lay, lay_o), (dgate, dgate_o), (slot_s, slot_o))):
+        outs.append(pltpu.make_async_copy(src, dst, out_sem.at[3 + i]))
+        outs[-1].start()
     crs[2].wait_recv()
     find[...] += crsd_r[...].astype(F32)
     outs.append(pltpu.make_async_copy(find, gd_o, out_sem.at[2]))
@@ -326,10 +350,6 @@
         outs[-1].start()
 
     arrived(3, xs, dxr)
-    unpack(dxr)
-    both = p0 + p1
-    for p in range(NP):
-        dtok_o[:, p * PC : (p + 1) * PC] = mm(both, X[p]).astype(BF16)
 
     sent(1, gs)
     sent(2, os_)
@@ -345,6 +365,50 @@
         o.wait()
 
 
+def finish(
+    cap,
+    slots, dxr, lay, dgate, gg, gu, gd,
+    dtok_o, lay_o, dgate_o, gg_o, gu_o, gd_o,
+    got, dtok, scr, Y, gg_v, gu_v, gd_v, lay_v, dgate_v, got_sem, in_sem, out_sem, dtok_sem,
+):
+    T, D = dtok.shape
+    S, ROWS, _ = got.shape
+    NP, _, PC = Y.shape
+    step = 16 * cap
+    loads = []
+    for c in range(S // step):
+        rows = pl.ds(c * step, step)
+        loads.append(pltpu.make_async_copy(dxr.at[rows], got.at[rows], got_sem.at[c]))
+        loads[-1].start()
+    through = ((gg, gg_v, gg_o), (gu, gu_v, gu_o), (gd, gd_v, gd_o), (lay, lay_v, lay_o), (dgate, dgate_v, dgate_o))
+    copies = []
+    for i, (src, held, dst) in enumerate(through):
+        copies.append(pltpu.make_async_copy(src, held, in_sem.at[i]))
+        copies[-1].start()
+    stores = []
+    for c in range(S // step):
+        loads[c].wait()
+        rows = pl.ds(c * step, step)
+        scr[...] = got[rows].astype(F32).reshape(step * ROWS, LANE)
+        for j in range(ROWS):
+            p, o = divmod(j * LANE, PC)
+            Y[p, rows, o : o + LANE] = scr[pl.ds(j, step, stride=ROWS), :].astype(BF16)
+        while len(stores) < min(2 * c, len(through)):
+            i = len(stores)
+            copies[i].wait()
+            stores.append(pltpu.make_async_copy(*through[i][1:], out_sem.at[i]))
+            stores[-1].start()
+    iota = lax.broadcasted_iota(jnp.int32, (T, S), 1)
+    both = jnp.where((slots[:, 0:1] == iota) | (slots[:, 1:2] == iota), 1.0, 0.0).astype(BF16)
+    for p in range(NP):
+        dtok[:, p * PC : (p + 1) * PC] = mm(both, Y[p]).astype(BF16)
+    out = pltpu.make_async_copy(dtok, dtok_o, dtok_sem)
+    out.start()
+    for c in stores:
+        c.wait()
+    out.wait()
+
+
 def on_device(tokens, routes, gate_probs, cotangent, w_gate, w_up, w_down):
     T, D = tokens.shape
     E = lax.axis_size("expert")
@@ -353,14 +417,21 @@
     cap = max(2, 3 * T * routes.shape[1] // (2 * E))
     S = E * cap
     ROWS = D // LANE
-    slots = pltpu.VMEM((S, ROWS, LANE), BF16)
+    rows_buf = pltpu.VMEM((S, ROWS, LANE), BF16)
     dma = pltpu.SemaphoreType.DMA
     vmem = pl.BlockSpec(memory_space=pltpu.VMEM)
     hbm = pl.BlockSpec(memory_space=pl.ANY)
     scratch = [
+        pltpu.VMEM((T, D), BF16),
+        pltpu.VMEM((2, T), jnp.int32),
+        pltpu.VMEM((2, T), F32),
+        pltpu.VMEM((T, D), BF16),
+        pltpu.VMEM((T, 2), F32),
+        pltpu.VMEM((T, D), BF16),
+        pltpu.VMEM((2, T), F32),
         pltpu.VMEM((T, 2), jnp.int32),
         pltpu.VMEM((2 * T, D), BF16),
-        *([slots] * 7),
+        *([rows_buf] * 6),
         pltpu.VMEM((NP, S, PC), BF16),
         pltpu.VMEM((NP, PC, S), BF16),
         pltpu.VMEM((FF, S), BF16),
@@ -383,26 +454,54 @@
         pltpu.VMEM((FF, PC), F32),
         dma((4,)), dma((4,)), dma((4,)),
         dma((3,)), dma((6,)), dma((3,)), dma((3,)), dma((3,)), dma((3,)),
-        dma((3, 2)), dma((3, 2)), dma((3,)), dma((3,)), dma((3,)),
+        dma((3, 2)), dma((3, 2)), dma((3,)), dma((3,)), dma((4,)), dma((6,)),
     ]
-    lay, dtok, dgates, gg, gu, gd = pl.pallas_call(
+    lay_shape = jax.ShapeDtypeStruct((T, D), BF16)
+    dgate_shape = jax.ShapeDtypeStruct((2, T), F32)
+    grads = (
+        jax.ShapeDtypeStruct((PC, FF), F32),
+        jax.ShapeDtypeStruct((PC, FF), F32),
+        jax.ShapeDtypeStruct((FF, PC), F32),
+    )
+    lay, dgate, slots, dxr, gg, gu, gd = pl.pallas_call(
         functools.partial(kernel, cap),
         out_shape=(
-            jax.ShapeDtypeStruct((T, D), BF16),
-            jax.ShapeDtypeStruct((T, D), BF16),
-            jax.ShapeDtypeStruct((T, 2), F32),
-            jax.ShapeDtypeStruct((PC, FF), F32),
-            jax.ShapeDtypeStruct((PC, FF), F32),
-            jax.ShapeDtypeStruct((FF, PC), F32),
+            lay_shape,
+            dgate_shape,
+            jax.ShapeDtypeStruct((T, 2), jnp.int32),
+            jax.ShapeDtypeStruct((S, ROWS, LANE), BF16),
+            *grads,
         ),
-        in_specs=[vmem, vmem, vmem, vmem, hbm, hbm, hbm],
-        out_specs=(vmem, vmem, vmem, hbm, hbm, hbm),
+        in_specs=[hbm] * 7,
+        out_specs=(hbm,) * 7,
         scratch_shapes=scratch,
         compiler_params=pltpu.CompilerParams(
             collective_id=0, has_side_effects=True, vmem_limit_bytes=64000 * 1024
         ),
-    )(tokens, routes, gate_probs, cotangent, w_gate[0], w_up[0], w_down[0])
-    return lay, dtok, dgates, gg[None], gu[None], gd[None]
+    )(tokens, routes.T, gate_probs.T, cotangent, w_gate[0], w_up[0], w_down[0])
+    dtok, lay, dgate, gg, gu, gd = pl.pallas_call(
+        functools.partial(finish, cap),
+        out_shape=(lay_shape, lay_shape, dgate_shape, *grads),
+        in_specs=[vmem] + [hbm] * 6,
+        out_specs=(hbm,) * 6,
+        scratch_shapes=[
+            pltpu.VMEM((S, ROWS, LANE), BF16),
+            pltpu.VMEM((T, D), BF16),
+            pltpu.VMEM((16 * cap * ROWS, LANE), F32),
+            pltpu.VMEM((NP, S, PC), BF16),
+            pltpu.VMEM((PC, FF), F32),
+            pltpu.VMEM((PC, FF), F32),
+            pltpu.VMEM((FF, PC), F32),
+            pltpu.VMEM((T, D), BF16),
+            pltpu.VMEM((2, T), F32),
+            dma((S // (16 * cap),)),
+            dma((5,)),
+            dma((5,)),
+            dma,
+        ],
+        compiler_params=pltpu.CompilerParams(vmem_limit_bytes=64000 * 1024),
+    )(slots, dxr, lay, dgate, gg, gu, gd)
+    return lay, dtok, dgate.T, gg[None], gu[None], gd[None]
 
 
 def solution(mesh):

time: 194 us -> 182 us (0.938)
  local copies, waits for them, and re-layouts: 13.6 us -> 0 us
    unnamed x14 -> x0, local copies, waits for them, and re-layouts: 13.6 us -> none
    pallas_call x1 -> x2, Pallas kernels: 180 us -> 181 us  [the longest x1 175 us: on_device(): pl.pallas_call(functools.partial(kernel, cap), out_shape=(lay_shape, dgat...]
where the time goes in v2:
time: 182 us
  Pallas kernels  181 us (99%)
    pallas_call x1, Pallas kernels, on_device(): pl.pallas_call(functools.partial(kernel, cap), out_shape=(lay_shape, dgat...  175 us
    pallas_call x1, Pallas kernels, on_device(): pl.pallas_call(functools.partial(finish, cap), out_shape=(lay_shape, lay_...  6.07 us

profile of v2, /device:TPU:1, one launch (start us, length us, event | category | flops | bytes accessed | tf_op | source)
XLA Modules:
  0.0 182.0 jit_solution(7541019879324131058)
XLA Ops:
  0.6 175.1 %shard_map.118 = (bf16[160,2048]{1,0:T(8,128)(2,1)}, f32[2,160]{1,0:T(2,128)}, s32[160,2]{1,0:T(8,128)}, bf16[448,16,128]{2,1,0:T(8,128)(2,1)}, f32[512,768]{1,0...) custom-call(bf16[160,2048]{1,0:T(8,128)(2,1)} %tok_in.1, s32[2,160]{1,0:T(2,128)} %bitcast.12, f32[2,160]{1,0:T(2,128)} %bitcast.13, ...), custom_call_target="tpu_custom_call" | custom-call | tf_op jit(solution)/shard_map/pallas_call | solution.py:466
  175.7 6.1 %shard_map.119 = (bf16[160,2048]{1,0:T(8,128)(2,1)}, bf16[160,2048]{1,0:T(8,128)(2,1)}, f32[2,160]{1,0:T(2,128)}, f32[512,768]{1,0:T(8,128)}, f32[512,768]{1,0:T(8,128)}, /*index=5*/f32[768,512]{1,0:T(8,128)}) custom-call(s32[160,2]{1,0:T(8,128)} %get-tuple-element.19.slots, bf16[448,16,128]{2,1,0:T(8,128)(2,1)} %get-tuple-element.20.dxr, ...), custom_call_target="tpu_custom_call" | custom-call | tf_op jit(solution)/shard_map/pallas_call | solution.py:482

commit v3 on v2

--- a/solution.py
+++ b/solution.py
@@ -32,12 +32,12 @@
     cap,
     tok_in, routes_in, probs_in, cot_in, wg_in, wu_in, wd_in,
     lay_o, dgate_o, slot_o, dxr, gg_o, gu_o, gd_o,
-    tok, routes, probs_t, cot, probs, lay, dgate, slot_s, rg, xs, gs, os_, xr, gr, orr, X, XT, HT, WG, WU, WD, A, B, HID, DG, DU, scr,
+    toks, rts, prb, cots, lay, dgate, slot_s, rg, xs, gs, os_, xr, gr, orr, X, XT, HT, WG, WU, WD, A, B, HID, DG, DU, scr,
     sib_s, sib_r, sibd_s, sibd_r, crs_s, crs_r, crsd_s, crsd_r, fin, find,
     a2a_send, a2a_recv, a2a_loc, ag_loc, ag_send, ag_cross, ag_sib, ag_fwd_s, ag_fwd_r,
-    sib_ss, sib_rs, crs_ss, crs_rs, in_sem, out_sem,
+    sib_ss, sib_rs, crs_ss, crs_rs, in_sem, out_sem, near_s, near_r,
 ):
-    T, D = tok.shape
+    _, T, D = toks.shape
     E = lax.axis_size("expert")
     NZ = E // PLANE
     S = E * cap
@@ -65,13 +65,13 @@
         pl.semaphore_signal(barrier, inc=1, device_id=partner(lax.div(k, PLANE), lax.rem(k, PLANE)), device_id_type=MESH)
         return carry
 
-    lax.fori_loop(1, E, greet, 0)
+    lax.fori_loop(1, E, greet, 0, unroll=7)
     pl.semaphore_signal(barrier, inc=1, device_id=sibling, device_id_type=MESH)
     pl.semaphore_signal(barrier, inc=1, device_id=across, device_id_type=MESH)
 
     ins = []
-    for i, (src, dst) in enumerate(((routes_in, routes), (probs_in, probs_t), (tok_in, tok), (cot_in, cot))):
-        ins.append(pltpu.make_async_copy(src, dst, in_sem.at[i]))
+    for i, (src, dst) in enumerate(((routes_in, rts), (probs_in, prb), (tok_in, toks), (cot_in, cots))):
+        ins.append(pltpu.make_async_copy(src, dst.at[0], in_sem.at[i]))
         ins[-1].start()
 
     eye = lax.broadcasted_iota(jnp.int32, (T, T), 0) == lax.broadcasted_iota(jnp.int32, (T, T), 1)
@@ -79,66 +79,109 @@
     def column(row):
         return jnp.sum(jnp.where(eye, row, jnp.zeros_like(row)), axis=1, keepdims=True)
 
-    ins[0].wait()
-    r0, r1 = column(routes[0:1, :]), column(routes[1:2, :])
     iota_e = lax.broadcasted_iota(jnp.int32, (T, E), 1)
-    h0, h1 = r0 == iota_e, r1 == iota_e
-    hits = (jnp.where(h0, 1.0, 0.0) + jnp.where(h1, 1.0, 0.0)).astype(BF16)
     tri = jnp.where(
         lax.broadcasted_iota(jnp.int32, (T, T), 0) > lax.broadcasted_iota(jnp.int32, (T, T), 1), 1.0, 0.0
     ).astype(BF16)
-    before = mm(tri, hits)
-    for k, (r, h) in enumerate(((r0, h0), (r1, h1))):
-        rank = jnp.sum(jnp.where(h, before, 0.0), axis=1, keepdims=True).astype(jnp.int32)
-        slot_s[:, k : k + 1] = jnp.where(rank < cap, r * cap + rank, S)
-
-    def send_block(a, src, dst, dz, i):
+
+    def find_slots(s):
+        r0, r1 = column(rts[s, 0:1, :]), column(rts[s, 1:2, :])
+        h0, h1 = r0 == iota_e, r1 == iota_e
+        hits = (jnp.where(h0, 1.0, 0.0) + jnp.where(h1, 1.0, 0.0)).astype(BF16)
+        before = mm(tri, hits)
+        for k, (r, h) in enumerate(((r0, h0), (r1, h1))):
+            rank = jnp.sum(jnp.where(h, before, 0.0), axis=1, keepdims=True).astype(jnp.int32)
+            slot_s[s, :, k : k + 1] = jnp.where(rank < cap, r * cap + rank, S)
+
+    def find_route_grads(s):
+        for k in range(2):
+            rg[k * T : (k + 1) * T, :] = (column(prb[s, k : k + 1, :]) * cots[s].astype(F32)).astype(BF16)
+
+    def send_block(a, src, row, dst, owner, dz, i):
         d, e = partner(dz, i)
         pltpu.make_async_remote_copy(
-            src.at[pl.ds(e * cap, cap)],
-            dst.at[pl.ds(me * cap, cap)],
+            src.at[pl.ds(row + lax.rem(e, PLANE) * cap, cap)],
+            dst.at[pl.ds(owner * cap, cap)],
             a2a_send.at[a],
             a2a_recv.at[a],
             device_id=(d, e),
             device_id_type=MESH,
         ).start()
 
-    def exchange(a, fill, src, dst, filled=False):
-        def send_plane(dz):
-            def one(i, c):
-                send_block(a, src, dst, dz, i)
-                return c
-
-            lax.fori_loop(0, PLANE, one, 0)
-
+    def keep_block(a, src, row, dst, owner):
+        pltpu.make_async_copy(
+            src.at[pl.ds(row + lax.rem(me, PLANE) * cap, cap)], dst.at[pl.ds(owner * cap, cap)], a2a_loc.at[a]
+        ).start()
+
+    def own_plane(a, src, row, dst):
+        keep_block(a, src, row, dst, me)
+
+        def one(i, c):
+            send_block(a, src, row, dst, me, 0, i)
+            return c
+
+        lax.fori_loop(1, PLANE, one, 0)
+
+    def exchange(a, fill, src, dst):
         def plane(q, carry):
             half = lax.div(q + 1, 2)
             dz = lax.rem(NZ // 2 + half * (2 * lax.rem(q, 2) - 1), NZ)
-            fill(lax.rem(my_z + dz, NZ) * CH)
-            send_plane(dz)
+            row = lax.rem(my_z + dz, NZ) * CH
+            fill(row)
+
+            def one(i, c):
+                send_block(a, src, row, dst, me, dz, i)
+                return c
+
+            lax.fori_loop(0, PLANE, one, 0)
             return carry
 
-        if filled:
-            send_plane(NZ // 2)
-        lax.fori_loop(1 if filled else 0, NZ - 1, plane, 0)
+        lax.fori_loop(0, NZ - 1, plane, 0)
         fill(my_z * CH)
-        mine = pl.ds(me * cap, cap)
-        pltpu.make_async_copy(src.at[mine], dst.at[mine], a2a_loc.at[a]).start()
-
-        def rest(i, c):
-            send_block(a, src, dst, 0, i)
-            return c
-
-        lax.fori_loop(1, PLANE, rest, 0)
-
-    def arrived(a, src, dst):
-        block = dst.at[pl.ds(0, S - cap)]
+        own_plane(a, src, my_z * CH, dst)
+
+    def relay(a, prepare, fill, src, dst):
+        def side(d, carry):
+            prepare(d)
+            way = 1 - 2 * d
+            owner = lax.rem(my_z + NZ - way, NZ) * PLANE + lax.rem(me, PLANE)
+
+            def plane(t, c0):
+                q = NZ // 2 - 1 - t
+                dz = lax.rem(NZ + way * q, NZ)
+                row = (1 + (NZ // 2) * d + q) * CH
+                fill(1 + d, lax.rem(my_z + dz, NZ) * CH, row)
+
+                def one(i, c1):
+                    other_half = (q == NZ // 2 - 1) & (lax.rem(my_x + i, 2) != d)
+                    stays = (q == 0) & (i == 0)
+
+                    @pl.when(stays)
+                    def _():
+                        keep_block(a, src, row, dst, owner)
+
+                    @pl.when(jnp.logical_not(stays | other_half))
+                    def _():
+                        send_block(a, src, row, dst, owner, dz, i)
+
+                    return c1
+
+                lax.fori_loop(0, PLANE, one, 0)
+                return c0
+
+            lax.fori_loop(0, NZ // 2, plane, 0)
+            return carry
+
+        lax.fori_loop(0, 2, side, 0)
+
+    def arrived(a, dst, kept):
+        block = dst.at[pl.ds(0, S - kept * cap)]
         pltpu.make_async_copy(block, block, a2a_recv.at[a]).wait()
-        mine = pl.ds(me * cap, cap)
-        pltpu.make_async_copy(src.at[mine], dst.at[mine], a2a_loc.at[a]).wait()
-
-    def sent(a, src):
-        block = src.at[pl.ds(0, S - cap)]
+        block = dst.at[pl.ds(0, kept * cap)]
+        pltpu.make_async_copy(block, block, a2a_loc.at[a]).wait()
+
+    def sent(a, src, kept):
+        block = src.at[pl.ds(0, S - kept * cap)]
         pltpu.make_async_copy(block, block, a2a_send.at[a]).wait()
 
     def lay_rows(v, dst, base):
@@ -146,24 +189,41 @@
             scr[pl.ds(j, CH, stride=ROWS), :] = v[:, j * LANE : (j + 1) * LANE]
         dst[pl.ds(base, CH)] = scr[pl.ds(0, CH * ROWS), :].reshape(CH, ROWS, LANE).astype(BF16)
 
-    def onehot(k, base, n):
+    def onehot(k, base, n, s=0):
         return jnp.where(
-            slot_s[:, k : k + 1] == lax.broadcasted_iota(jnp.int32, (T, n), 1) + base, 1.0, 0.0
+            slot_s[s, :, k : k + 1] == lax.broadcasted_iota(jnp.int32, (T, n), 1) + base, 1.0, 0.0
         )
 
-    def fill_x(base):
-        pick = (onehot(0, base, CH) + onehot(1, base, CH)).astype(BF16)
-        lay_rows(mm_first(pick, tok[...]), xs, base)
-
-    def fill_g(base):
-        v = mm_first(onehot(0, base, CH).astype(BF16), rg[0:T, :])
-        v += mm_first(onehot(1, base, CH).astype(BF16), rg[T : 2 * T, :])
-        lay_rows(v, gs, base)
-
-    first = lax.rem(my_z + NZ // 2, NZ) * CH
-    ins[2].wait()
-    fill_x(first)
+    def fill_x(s, base, row):
+        pick = (onehot(0, base, CH, s) + onehot(1, base, CH, s)).astype(BF16)
+        lay_rows(mm_first(pick, toks[s]), xs, row)
+
+    def fill_g(s, base, row):
+        v = mm_first(onehot(0, base, CH, s).astype(BF16), rg[0:T, :])
+        v += mm_first(onehot(1, base, CH, s).astype(BF16), rg[T : 2 * T, :])
+        lay_rows(v, gs, row)
+
+    def to_neighbours(kind, src, buf):
+        copies = []
+        for d in range(2):
+            c = pltpu.make_async_remote_copy(
+                src,
+                buf.at[1 + d],
+                near_s.at[kind, d],
+                near_r.at[kind, d],
+                device_id=partner((1, NZ - 1)[d], 0),
+                device_id_type=MESH,
+            )
+            c.start()
+            copies.append(c)
+        return copies
+
+    def from_neighbour(kind, buf, d):
+        pltpu.make_async_copy(buf.at[1 + d], buf.at[1 + d], near_r.at[kind, d]).wait()
+
     pl.semaphore_wait(barrier, E + 1)
+    near = to_neighbours(0, routes_in, rts) + to_neighbours(2, tok_in, toks) + to_neighbours(1, probs_in, prb)
+
     mats = ((wg_in, WG), (wu_in, WU), (wd_in, WD))
     ag = []
     for m, (src, full) in enumerate(mats):
@@ -179,13 +239,30 @@
         l.start()
         ag.append((c, s, l))
 
-    exchange(0, fill_x, xs, xr, True)
+    near += to_neighbours(3, cot_in, cots)
+    ins[0].wait()
+    find_slots(0)
+    ins[2].wait()
+    fill_x(0, my_z * CH, 0)
+    own_plane(0, xs, 0, xr)
     ins[1].wait()
     ins[3].wait()
-    for k in range(2):
-        probs[:, k : k + 1] = column(probs_t[k : k + 1, :])
-        rg[k * T : (k + 1) * T, :] = (probs[:, k : k + 1] * cot[...].astype(F32)).astype(BF16)
-    exchange(1, fill_g, gs, gr)
+    find_route_grads(0)
+    fill_g(0, my_z * CH, 0)
+    own_plane(1, gs, 0, gr)
+
+    def prepare_x(d):
+        from_neighbour(0, rts, d)
+        find_slots(1 + d)
+        from_neighbour(2, toks, d)
+
+    def prepare_g(d):
+        from_neighbour(1, prb, d)
+        from_neighbour(3, cots, d)
+        find_route_grads(1 + d)
+
+    relay(0, prepare_x, fill_x, xs, xr)
+    relay(1, prepare_g, fill_g, gs, gr)
 
     def forward_weights(m):
         full = mats[m][1]
@@ -215,7 +292,7 @@
         lax.fori_loop(0, S // step, chunk, 0)
 
     fwd = [forward_weights(0), forward_weights(1)]
-    arrived(0, xs, xr)
+    arrived(0, xr, 3)
     unpack(xr)
     weights_here(0, fwd[0])
     weights_here(1, fwd[1])
@@ -258,7 +335,7 @@
         XT[p] = X[p].T
     HT[...] = HID[...].T
 
-    arrived(1, gs, gr)
+    arrived(1, gr, 3)
     unpack(gr)
 
     def to_sibling(k, buf_s, buf_r, s):
@@ -311,7 +388,7 @@
         crs_s[m] = (part_gu(m, crs_dp) + sib_r[m, 1 - xlo].astype(F32)).astype(BF16)
         crs[m] = to_across(m, crs_s.at[m], crs_r.at[m])
 
-    sent(0, xs)
+    sent(0, xs, 3)
     for p in range(NP):
         rows_out(p, mm_last(DG[...], WG[p]) + mm_last(DU[...], WU[p]))
     exchange(3, fill_from_scr(xs), xs, dxr)
@@ -320,23 +397,24 @@
     for m in range(2):
         fin[m] = part_gu(m, dp) + sib_r[m, xlo].astype(F32)
 
-    arrived(2, os_, orr)
+    arrived(2, orr, 1)
     unpack(orr)
     p0, p1 = onehot(0, 0, S).astype(BF16), onehot(1, 0, S).astype(BF16)
+    w0, w1 = column(prb[0, 0:1, :]), column(prb[0, 1:2, :])
     dg0 = jnp.zeros((T, 1), F32)
     dg1 = jnp.zeros((T, 1), F32)
     for p in range(NP):
         cols = slice(p * PC, (p + 1) * PC)
         k0, k1 = mm(p0, X[p]), mm(p1, X[p])
-        lay[:, cols] = (probs[:, 0:1] * k0 + probs[:, 1:2] * k1).astype(BF16)
-        c32 = cot[:, cols].astype(F32)
+        lay[:, cols] = (w0 * k0 + w1 * k1).astype(BF16)
+        c32 = cots[0, :, cols].astype(F32)
         dg0 += jnp.sum(c32 * k0, axis=1, keepdims=True)
         dg1 += jnp.sum(c32 * k1, axis=1, keepdims=True)
     for k, v in enumerate((dg0, dg1)):
         dgate[k : k + 1, :] = jnp.sum(jnp.where(eye, v, 0.0), axis=0, keepdims=True)
 
     outs = []
-    for i, (src, dst) in enumerate(((lay, lay_o), (dgate, dgate_o), (slot_s, slot_o))):
+    for i, (src, dst) in enumerate(((lay, lay_o), (dgate, dgate_o), (slot_s.at[0], slot_o))):
         outs.append(pltpu.make_async_copy(src, dst, out_sem.at[3 + i]))
         outs[-1].start()
     crs[2].wait_recv()
@@ -349,11 +427,13 @@
         outs.append(pltpu.make_async_copy(fin.at[m], o, out_sem.at[m]))
         outs[-1].start()
 
-    arrived(3, xs, dxr)
-
-    sent(1, gs)
-    sent(2, os_)
-    sent(3, xs)
+    arrived(3, dxr, 1)
+
+    sent(1, gs, 3)
+    sent(2, os_, 1)
+    sent(3, xs, 1)
+    for c in near:
+        c.wait_send()
     for m in range(3):
         ag[m][0].wait_send()
         ag[m][1].wait_send()
@@ -418,20 +498,21 @@
     S = E * cap
     ROWS = D // LANE
     rows_buf = pltpu.VMEM((S, ROWS, LANE), BF16)
+    relay_buf = pltpu.VMEM((S + PLANE * cap, ROWS, LANE), BF16)
     dma = pltpu.SemaphoreType.DMA
     vmem = pl.BlockSpec(memory_space=pltpu.VMEM)
     hbm = pl.BlockSpec(memory_space=pl.ANY)
     scratch = [
-        pltpu.VMEM((T, D), BF16),
-        pltpu.VMEM((2, T), jnp.int32),
-        pltpu.VMEM((2, T), F32),
-        pltpu.VMEM((T, D), BF16),
-        pltpu.VMEM((T, 2), F32),
+        pltpu.VMEM((3, T, D), BF16),
+        pltpu.VMEM((3, 2, T), jnp.int32),
+        pltpu.VMEM((3, 2, T), F32),
+        pltpu.VMEM((3, T, D), BF16),
         pltpu.VMEM((T, D), BF16),
         pltpu.VMEM((2, T), F32),
-        pltpu.VMEM((T, 2), jnp.int32),
+        pltpu.VMEM((3, T, 2), jnp.int32),
         pltpu.VMEM((2 * T, D), BF16),
-        *([rows_buf] * 6),
+        *([relay_buf] * 2),
+        *([rows_buf] * 4),
         pltpu.VMEM((NP, S, PC), BF16),
         pltpu.VMEM((NP, PC, S), BF16),
         pltpu.VMEM((FF, S), BF16),
@@ -454,7 +535,7 @@
         pltpu.VMEM((FF, PC), F32),
         dma((4,)), dma((4,)), dma((4,)),
         dma((3,)), dma((6,)), dma((3,)), dma((3,)), dma((3,)), dma((3,)),
-        dma((3, 2)), dma((3, 2)), dma((3,)), dma((3,)), dma((4,)), dma((6,)),
+        dma((3, 2)), dma((3, 2)), dma((3,)), dma((3,)), dma((4,)), dma((6,)), dma((4, 2)), dma((4, 2)),
     ]
     lay_shape = jax.ShapeDtypeStruct((T, D), BF16)
     dgate_shape = jax.ShapeDtypeStruct((2, T), F32)

time: 182 us -> 174 us (0.956)
  Pallas kernels: 181 us -> 173 us
    pallas_call x1, Pallas kernels: 175 us -> 167 us  [on_device(): pl.pallas_call(functools.partial(kernel, cap), out_shape=(lay_shape, dgat...]
where the time goes in v3:
time: 174 us
  Pallas kernels  173 us (99%)
    pallas_call x1, Pallas kernels, on_device(): pl.pallas_call(functools.partial(kernel, cap), out_shape=(lay_shape, dgat...  167 us
    pallas_call x1, Pallas kernels, on_device(): pl.pallas_call(functools.partial(finish, cap), out_shape=(lay_shape, lay_...  6.07 us

profile of v3, /device:TPU:1, one launch (start us, length us, event | category | flops | bytes accessed | tf_op | source)
XLA Modules:
  0.0 174.0 jit_solution(3764594854577874108)
XLA Ops:
  0.6 167.1 %shard_map.118 = (bf16[160,2048]{1,0:T(8,128)(2,1)}, f32[2,160]{1,0:T(2,128)}, s32[160,2]{1,0:T(8,128)}, bf16[448,16,128]{2,1,0:T(8,128)(2,1)}, f32[512,768]{1,0...) custom-call(bf16[160,2048]{1,0:T(8,128)(2,1)} %tok_in.1, s32[2,160]{1,0:T(2,128)} %bitcast.12, f32[2,160]{1,0:T(2,128)} %bitcast.13, ...), custom_call_target="tpu_custom_call" | custom-call | tf_op jit(solution)/shard_map/pallas_call | solution.py:547
  167.8 6.1 %shard_map.119 = (bf16[160,2048]{1,0:T(8,128)(2,1)}, bf16[160,2048]{1,0:T(8,128)(2,1)}, f32[2,160]{1,0:T(2,128)}, f32[512,768]{1,0:T(8,128)}, f32[512,768]{1,0:T(8,128)}, /*index=5*/f32[768,512]{1,0:T(8,128)}) custom-call(s32[160,2]{1,0:T(8,128)} %get-tuple-element.19.slots, bf16[448,16,128]{2,1,0:T(8,128)(2,1)} %get-tuple-element.20.dxr, ...), custom_call_target="tpu_custom_call" | custom-call | tf_op jit(solution)/shard_map/pallas_call | solution.py:563

commit v4 on v3

--- a/solution.py
+++ b/solution.py
@@ -447,9 +447,9 @@
 
 def finish(
     cap,
-    slots, dxr, lay, dgate, gg, gu, gd,
+    slots_in, dxr, lay, dgate, gg, gu, gd,
     dtok_o, lay_o, dgate_o, gg_o, gu_o, gd_o,
-    got, dtok, scr, Y, gg_v, gu_v, gd_v, lay_v, dgate_v, got_sem, in_sem, out_sem, dtok_sem,
+    got, dtok, scr, Y, gg_v, gu_v, gd_v, lay_v, dgate_v, slots, got_sem, in_sem, out_sem, dtok_sem, slot_sem,
 ):
     T, D = dtok.shape
     S, ROWS, _ = got.shape
@@ -460,6 +460,8 @@
         rows = pl.ds(c * step, step)
         loads.append(pltpu.make_async_copy(dxr.at[rows], got.at[rows], got_sem.at[c]))
         loads[-1].start()
+    slot_load = pltpu.make_async_copy(slots_in, slots, slot_sem)
+    slot_load.start()
     through = ((gg, gg_v, gg_o), (gu, gu_v, gu_o), (gd, gd_v, gd_o), (lay, lay_v, lay_o), (dgate, dgate_v, dgate_o))
     copies = []
     for i, (src, held, dst) in enumerate(through):
@@ -469,7 +471,7 @@
     for c in range(S // step):
         loads[c].wait()
         rows = pl.ds(c * step, step)
-        scr[...] = got[rows].astype(F32).reshape(step * ROWS, LANE)
+        scr[pl.ds(0, step * ROWS), :] = got[rows].astype(F32).reshape(step * ROWS, LANE)
         for j in range(ROWS):
             p, o = divmod(j * LANE, PC)
             Y[p, rows, o : o + LANE] = scr[pl.ds(j, step, stride=ROWS), :].astype(BF16)
@@ -478,6 +480,7 @@
             copies[i].wait()
             stores.append(pltpu.make_async_copy(*through[i][1:], out_sem.at[i]))
             stores[-1].start()
+    slot_load.wait()
     iota = lax.broadcasted_iota(jnp.int32, (T, S), 1)
     both = jnp.where((slots[:, 0:1] == iota) | (slots[:, 1:2] == iota), 1.0, 0.0).astype(BF16)
     for p in range(NP):
@@ -500,7 +503,6 @@
     rows_buf = pltpu.VMEM((S, ROWS, LANE), BF16)
     relay_buf = pltpu.VMEM((S + PLANE * cap, ROWS, LANE), BF16)
     dma = pltpu.SemaphoreType.DMA
-    vmem = pl.BlockSpec(memory_space=pltpu.VMEM)
     hbm = pl.BlockSpec(memory_space=pl.ANY)
     scratch = [
         pltpu.VMEM((3, T, D), BF16),
@@ -522,7 +524,7 @@
         pltpu.VMEM((S, FF), F32),
         pltpu.VMEM((S, FF), F32),
         *([pltpu.VMEM((S, FF), BF16)] * 3),
-        pltpu.VMEM((S * ROWS, LANE), F32),
+        pltpu.VMEM((S * ROWS + 8 * ROWS, LANE), F32),
         pltpu.VMEM((2, 2, PC, FF), BF16),
         pltpu.VMEM((2, 2, PC, FF), BF16),
         pltpu.VMEM((2, FF, PC), BF16),
@@ -563,21 +565,23 @@
     dtok, lay, dgate, gg, gu, gd = pl.pallas_call(
         functools.partial(finish, cap),
         out_shape=(lay_shape, lay_shape, dgate_shape, *grads),
-        in_specs=[vmem] + [hbm] * 6,
+        in_specs=[hbm] * 7,
         out_specs=(hbm,) * 6,
         scratch_shapes=[
             pltpu.VMEM((S, ROWS, LANE), BF16),
             pltpu.VMEM((T, D), BF16),
-            pltpu.VMEM((16 * cap * ROWS, LANE), F32),
+            pltpu.VMEM((16 * cap * ROWS + 8 * ROWS, LANE), F32),
             pltpu.VMEM((NP, S, PC), BF16),
             pltpu.VMEM((PC, FF), F32),
             pltpu.VMEM((PC, FF), F32),
             pltpu.VMEM((FF, PC), F32),
             pltpu.VMEM((T, D), BF16),
             pltpu.VMEM((2, T), F32),
+            pltpu.VMEM((T, 2), jnp.int32),
             dma((S // (16 * cap),)),
             dma((5,)),
             dma((5,)),
+            dma,
             dma,
         ],
         compiler_params=pltpu.CompilerParams(vmem_limit_bytes=64000 * 1024),

time: 174 us -> 173 us (level)
  no operation moved by 1% of the time
where the time goes in v4:
time: 173 us
  Pallas kernels  172 us (99%)
    pallas_call x1, Pallas kernels, on_device(): pl.pallas_call(functools.partial(kernel, cap), out_shape=(lay_shape, dgat...  167 us
    pallas_call x1, Pallas kernels, on_device(): pl.pallas_call(functools.partial(finish, cap), out_shape=(lay_shape, lay_...  5.19 us

profile of v4, /device:TPU:1, one launch (start us, length us, event | category | flops | bytes accessed | tf_op | source)
XLA Modules:
  0.0 173.1 jit_solution(7380805632260772184)
XLA Ops:
  0.6 167.1 %shard_map.118 = (bf16[160,2048]{1,0:T(8,128)(2,1)}, f32[2,160]{1,0:T(2,128)}, s32[160,2]{1,0:T(8,128)}, bf16[448,16,128]{2,1,0:T(8,128)(2,1)}, f32[512,768]{1,0...) custom-call(bf16[160,2048]{1,0:T(8,128)(2,1)} %tok_in.1, s32[2,160]{1,0:T(2,128)} %bitcast.12, f32[2,160]{1,0:T(2,128)} %bitcast.13, ...), custom_call_target="tpu_custom_call" | custom-call | tf_op jit(solution)/shard_map/pallas_call | solution.py:549
  167.8 5.2 %shard_map.119 = (bf16[160,2048]{1,0:T(8,128)(2,1)}, bf16[160,2048]{1,0:T(8,128)(2,1)}, f32[2,160]{1,0:T(2,128)}, f32[512,768]{1,0:T(8,128)}, f32[512,768]{1,0:T(8,128)}, /*index=5*/f32[768,512]{1,0:T(8,128)}) custom-call(s32[160,2]{1,0:T(8,128)} %get-tuple-element.19.slots_in, bf16[448,16,128]{2,1,0:T(8,128)(2,1)} %get-tuple-element.20.dxr, ...), custom_call_target="tpu_custom_call" | custom-call | tf_op jit(solution)/shard_map/pallas_call | solution.py:565

commit v5 on v4

--- a/solution.py
+++ b/solution.py
@@ -418,13 +418,13 @@
         outs.append(pltpu.make_async_copy(src, dst, out_sem.at[3 + i]))
         outs[-1].start()
     crs[2].wait_recv()
-    find[...] += crsd_r[...].astype(F32)
-    outs.append(pltpu.make_async_copy(find, gd_o, out_sem.at[2]))
+    crsd_r[...] = (find[...] + crsd_r[...].astype(F32)).astype(BF16)
+    outs.append(pltpu.make_async_copy(crsd_r, gd_o, out_sem.at[2]))
     outs[-1].start()
     for m, o in enumerate((gg_o, gu_o)):
         crs[m].wait_recv()
-        fin[m] += crs_r[m].astype(F32)
-        outs.append(pltpu.make_async_copy(fin.at[m], o, out_sem.at[m]))
+        crs_r[m] = (fin[m] + crs_r[m].astype(F32)).astype(BF16)
+        outs.append(pltpu.make_async_copy(crs_r.at[m], o, out_sem.at[m]))
         outs[-1].start()
 
     arrived(3, dxr, 1)
@@ -449,7 +449,7 @@
     cap,
     slots_in, dxr, lay, dgate, gg, gu, gd,
     dtok_o, lay_o, dgate_o, gg_o, gu_o, gd_o,
-    got, dtok, scr, Y, gg_v, gu_v, gd_v, lay_v, dgate_v, slots, got_sem, in_sem, out_sem, dtok_sem, slot_sem,
+    got, dtok, scr, Y, gg_v, gu_v, gd_v, lay_v, dgate_v, slots, gg_w, gu_w, gd_w, got_sem, in_sem, out_sem, dtok_sem, slot_sem,
 ):
     T, D = dtok.shape
     S, ROWS, _ = got.shape
@@ -463,6 +463,7 @@
     slot_load = pltpu.make_async_copy(slots_in, slots, slot_sem)
     slot_load.start()
     through = ((gg, gg_v, gg_o), (gu, gu_v, gu_o), (gd, gd_v, gd_o), (lay, lay_v, lay_o), (dgate, dgate_v, dgate_o))
+    wide = (gg_w, gu_w, gd_w)
     copies = []
     for i, (src, held, dst) in enumerate(through):
         copies.append(pltpu.make_async_copy(src, held, in_sem.at[i]))
@@ -475,10 +476,14 @@
         for j in range(ROWS):
             p, o = divmod(j * LANE, PC)
             Y[p, rows, o : o + LANE] = scr[pl.ds(j, step, stride=ROWS), :].astype(BF16)
-        while len(stores) < min(2 * c, len(through)):
+        while len(stores) < min(2 * c + 1, len(through)):
             i = len(stores)
             copies[i].wait()
-            stores.append(pltpu.make_async_copy(*through[i][1:], out_sem.at[i]))
+            held = through[i][1]
+            if i < len(wide):
+                wide[i][...] = held[...].astype(F32)
+                held = wide[i]
+            stores.append(pltpu.make_async_copy(held, through[i][2], out_sem.at[i]))
             stores[-1].start()
     slot_load.wait()
     iota = lax.broadcasted_iota(jnp.int32, (T, S), 1)
@@ -553,7 +558,7 @@
             dgate_shape,
             jax.ShapeDtypeStruct((T, 2), jnp.int32),
             jax.ShapeDtypeStruct((S, ROWS, LANE), BF16),
-            *grads,
+            *(jax.ShapeDtypeStruct(g.shape, BF16) for g in grads),
         ),
         in_specs=[hbm] * 7,
         out_specs=(hbm,) * 7,
@@ -572,12 +577,15 @@
             pltpu.VMEM((T, D), BF16),
             pltpu.VMEM((16 * cap * ROWS + 8 * ROWS, LANE), F32),
             pltpu.VMEM((NP, S, PC), BF16),
+            pltpu.VMEM((PC, FF), BF16),
+            pltpu.VMEM((PC, FF), BF16),
+            pltpu.VMEM((FF, PC), BF16),
+            pltpu.VMEM((T, D), BF16),
+            pltpu.VMEM((2, T), F32),
+            pltpu.VMEM((T, 2), jnp.int32),
             pltpu.VMEM((PC, FF), F32),
             pltpu.VMEM((PC, FF), F32),
             pltpu.VMEM((FF, PC), F32),
-            pltpu.VMEM((T, D), BF16),
-            pltpu.VMEM((2, T), F32),
-            pltpu.VMEM((T, 2), jnp.int32),
             dma((S // (16 * cap),)),
             dma((5,)),
             dma((5,)),

time: 173 us -> 173 us (level)
  no operation moved by 1% of the time
where the time goes in v5:
time: 173 us
  Pallas kernels  172 us (99%)
    pallas_call x1, Pallas kernels, on_device(): pl.pallas_call(functools.partial(kernel, cap), out_shape=(lay_shape, dgat...  167 us
    pallas_call x1, Pallas kernels, on_device(): pl.pallas_call(functools.partial(finish, cap), out_shape=(lay_shape, lay_...  4.58 us

profile of v5, /device:TPU:1, one launch (start us, length us, event | category | flops | bytes accessed | tf_op | source)
XLA Modules:
  0.0 172.5 jit_solution(580462567783997284)
XLA Ops:
  0.6 167.1 %shard_map.118 = (bf16[160,2048]{1,0:T(8,128)(2,1)}, f32[2,160]{1,0:T(2,128)}, s32[160,2]{1,0:T(8,128)}, bf16[448,16,128]{2,1,0:T(8,128)(2,1)}, bf16[512,768]{1,...) custom-call(bf16[160,2048]{1,0:T(8,128)(2,1)} %tok_in.1, s32[2,160]{1,0:T(2,128)} %bitcast.12, ...), custom_call_target="tpu_custom_call" | custom-call | tf_op jit(solution)/shard_map/pallas_call | solution.py:554
  167.8 4.6 %shard_map.119 = (bf16[160,2048]{1,0:T(8,128)(2,1)}, bf16[160,2048]{1,0:T(8,128)(2,1)}, f32[2,160]{1,0:T(2,128)}, f32[512,768]{1,0:T(8,128)}, f32[512,768]{1,0:T(8,128)}, /*index=5*/f32[768,512]{1,0:T(8,128)}) custom-call(s32[160,2]{1,0:T(8,128)} %get-tuple-element.19.slots_in, bf16[448,16,128]{2,1,0:T(8,128)(2,1)} %get-tuple-element.20.dxr, ...), custom_call_target="tpu_custom_call" | custom-call | tf_op jit(solution)/shard_map/pallas_call | solution.py:570
